TPU v7x, 32 devices: a whole 2x2x4 slice. The times are simulated.
32 devices in a mesh: expert: 4 (over y, x), context: 2 (over core), dp: 4 (over z).
Axes of the slice: x: 2, y: 2, z: 4, core: 2. Of those that a mesh axis runs over, the one named last changes fastest.
Arguments:
- tokens: bfloat16 [16, 2048, 768], P(('expert', 'dp'), 'context'), may hold values from -6 to 6
- segments: int32 [16, 2048], P(('expert', 'dp'), 'context'), may hold values from 0 to 4, as said below
- routes: int32 [16, 2048, 2], P(('expert', 'dp'), 'context'), may hold values from 0 to 7, all different within a row
- prev_logits: float32 [16, 2048, 8], P(('expert', 'dp'), 'context'), may hold values from -3 to 3
- ranks: int32 [16, 2, 1024], P(('expert', 'dp'), 'context'), may hold values from 0 to 1023, each once within a row
- cotangent: bfloat16 [16, 2048, 768], P(('expert', 'dp'), 'context'), may hold values from -6 to 6
- norm_one: bfloat16 [768], P('dp'), may hold values from 0.099609375 to 1.8984375
- w_query: bfloat16 [768, 768], P('dp'), may hold values from -0.21875 to 0.21875
- w_key: bfloat16 [768, 768], P('dp'), may hold values from -0.21875 to 0.21875
- w_value: bfloat16 [768, 768], P('dp'), may hold values from -0.21875 to 0.21875
- w_out: bfloat16 [768, 768], P('dp'), may hold values from -0.875 to 0.875
- norm_two: bfloat16 [768], P('dp'), may hold values from 0.099609375 to 1.8984375
- router: bfloat16 [768, 8], P('dp'), may hold values from -0.15625 to 0.15625
- w_res: bfloat16 [8, 8], replicated, may hold values from -2 to 2
- const_mix: bfloat16 [768, 4], P('dp'), may hold values from -0.21875 to 0.21875
- const_vec: bfloat16 [768, 2], P('dp'), may hold values from -5 to 5
- w_gate: bfloat16 [4, 768, 2048], P('expert', 'dp'), may hold values from -0.21875 to 0.21875
- w_up: bfloat16 [4, 768, 2048], P('expert', 'dp'), may hold values from -0.21875 to 0.21875
- w_down: bfloat16 [4, 2048, 768], P('expert', 'dp'), may hold values from -0.75 to 0.75
Outputs:
- output: bfloat16 [16, 2048, 768], P(('expert', 'dp'), 'context')
- grad_tokens: float32 [16, 2048, 768], P(('expert', 'dp'), 'context')
- grad_norm_one: float32 [768], P('dp')
- grad_w_query: float32 [768, 768], P('dp')
- grad_w_key: float32 [768, 768], P('dp')
- grad_w_value: float32 [768, 768], P('dp')
- grad_w_out: float32 [768, 768], P('dp')
- grad_norm_two: float32 [768], P('dp')
- grad_router: float32 [768, 8], P('dp')
- grad_w_res: float32 [8, 8], replicated
- grad_const_mix: float32 [768, 4], P('dp')
- grad_const_vec: float32 [768, 2], P('dp')
- grad_w_gate: float32 [4, 768, 2048], P('expert', 'dp')
- grad_w_up: float32 [4, 768, 2048], P('expert', 'dp')
- grad_w_down: float32 [4, 2048, 768], P('expert', 'dp')
Inputs may be any that keep to these rules, and one draw needn't show every extreme that they name: `segments`: segment numbers never fall along a sequence; the tokens with one number form one document. `routes`: each token names two different experts. In each block of 1024 consecutive tokens of a sequence the ranks are a permutation.
All inputs are finite; a program needn't handle non-finite values.
Results may differ from a plain program's by a relative error of at most 0.015.
Values may be sent and summed in bfloat16 or wider, within the bound.
A program may use at most 256 MiB of HBM per device.

v0:
```python
import functools

import jax
import jax.numpy as jnp
import numpy as np
from jax import lax
from jax.experimental import pallas as pl
from jax.experimental.pallas import tpu as pltpu
from jax.sharding import PartitionSpec as P

HEADS = 12
HEAD_DIM = 64
WIN = 1024
NZ = 4
GAIN_ONE, GAIN_TWO, VECS = 112, 113, 114
TQ = 256
TB = 256
FC = 256
LANES = 128
EPS = 1e-05
MASKED = -1000000000.0
HIGH = lax.Precision.HIGHEST
F32 = jnp.float32
BF16 = jnp.bfloat16
MIB = 1024 * 1024


def params(mib):
    return pltpu.CompilerParams(vmem_limit_bytes=mib * MIB)


def cost(flops, nbytes, trans=0):
    return pl.CostEstimate(flops=int(flops), bytes_accessed=int(nbytes), transcendentals=int(trans))


def dot(left, right):
    return jnp.dot(left, right, preferred_element_type=F32)


def dot_nt(left, right):
    return lax.dot_general(left, right, (((1,), (1,)), ((), ())), preferred_element_type=F32)


def dot_tn(left, right):
    return lax.dot_general(left, right, (((0,), (0,)), ((), ())), preferred_element_type=F32)


def iota(shape, axis):
    return lax.broadcasted_iota(jnp.int32, shape, axis)


def rope_tables(seq):
    half = HEAD_DIM // 2
    frequency = np.float32(10000.0) ** (
        -np.arange(half, dtype=np.float32) * np.float32(2.0) / np.float32(HEAD_DIM)
    )
    angles = np.arange(seq, dtype=np.float32)[:, None] * frequency.astype(np.float32)[None, :]
    cos = np.cos(angles.astype(np.float64)).astype(np.float32)
    sin = np.sin(angles.astype(np.float64)).astype(np.float32)
    return np.concatenate([cos] * 4, axis=1), np.concatenate([-sin, sin, -sin, sin], axis=1)


def swap_halves(chunk):
    lane = iota(chunk.shape, 1)
    return jnp.where(
        lane % HEAD_DIM < HEAD_DIM // 2, pltpu.roll(chunk, 96, 1), pltpu.roll(chunk, 32, 1)
    )


def loop(count, body):
    if count <= 4:
        for step in range(count):
            body(step)
    else:
        lax.fori_loop(0, count, lambda step, carry: (body(step), carry)[1], 0)


def remote(src, dst, sems, index, where):
    return pltpu.make_async_remote_copy(
        src_ref=src,
        dst_ref=dst,
        send_sem=sems.at[(0,) + index],
        recv_sem=sems.at[(1,) + index],
        device_id=where,
        device_id_type=pl.DeviceIdType.MESH,
    )


def greet_all(axes):
    barrier = pltpu.get_barrier_semaphore()
    total = 0
    for axis in axes:
        size = lax.axis_size(axis)
        me = lax.axis_index(axis)
        total += size - 1

        def greet(k, axis=axis, size=size, me=me):
            pl.semaphore_signal(
                barrier,
                inc=1,
                device_id={axis: lax.rem(me + k + 1, size)},
                device_id_type=pl.DeviceIdType.MESH,
            )

        loop(size - 1, greet)
    pl.semaphore_wait(barrier, total)


def spread_kernel(
    w_query_ref,
    w_key_ref,
    w_value_ref,
    w_out_ref,
    extra_ref,
    out_ref,
    extra_out_ref,
    slab_sems,
    plane_sems,
    core_sems,
    extra_sems,
):
    experts = lax.axis_size("expert")
    slabs = lax.axis_size("dp")
    me, core, slab = lax.axis_index("expert"), lax.axis_index("context"), lax.axis_index("dp")
    half = out_ref.shape[4]
    for which, ref in enumerate((w_query_ref, w_key_ref, w_value_ref, w_out_ref)):
        for side in range(2):

            @pl.when((me == which) & (core == side))
            def _():
                out_ref[which, side, slab] = ref[:, side * half : (side + 1) * half]

    extra_out_ref[slab] = extra_ref[...]
    greet_all(("context", "expert", "dp"))

    def slab_copy(k):
        piece = out_ref.at[me, core, slab]
        return remote(piece, piece, slab_sems, (k,), {"dp": lax.rem(slab + k + 1, slabs)})

    def extra_copy(k):
        piece = extra_out_ref.at[slab]
        return remote(piece, piece, extra_sems, (k,), {"dp": lax.rem(slab + k + 1, slabs)})

    def plane_copy(j, at):
        piece = out_ref.at[me, core, at]
        return remote(
            piece, piece, plane_sems, (j - 1, at), {"expert": lax.rem(me + j, experts)}
        )

    def core_copy(j, at):
        piece = out_ref.at[lax.rem(me + experts - j, experts), core, at]
        return remote(piece, piece, core_sems, (j, at), {"context": 1 - core})

    def share(at):
        for j in range(1, experts):
            plane_copy(j, at).start()
        core_copy(0, at).start()

    loop(slabs - 1, lambda k: extra_copy(k).start())
    loop(slabs - 1, lambda k: slab_copy(k).start())
    share(slab)

    def forward(k):
        slab_copy(k).wait_recv()
        share(lax.rem(slab + slabs - k - 1, slabs))

    loop(slabs - 1, forward)

    def relay(k):
        at = lax.rem(slab + slabs - k, slabs)
        for j in range(1, experts):
            plane_copy(j, at).wait_recv()
            core_copy(j, at).start()

    loop(slabs, relay)
    loop(slabs - 1, lambda k: extra_copy(k).wait())
    loop(slabs - 1, lambda k: slab_copy(k).wait_send())

    def finish(at):
        for j in range(experts):
            core_copy(j, at).wait()
        for j in range(1, experts):
            plane_copy(j, at).wait_send()

    loop(slabs, finish)


def spread(experts, slabs, w_query, w_key, w_value, w_out, extra):
    rows, width = w_query.shape
    half = width // 2
    vmem = pl.BlockSpec(memory_space=pltpu.VMEM)
    dma = pltpu.SemaphoreType.DMA
    return pl.pallas_call(
        spread_kernel,
        in_specs=[vmem] * 5,
        out_specs=[vmem] * 2,
        out_shape=(
            jax.ShapeDtypeStruct((4, 2, slabs, rows, half), BF16),
            jax.ShapeDtypeStruct((slabs,) + extra.shape, F32),
        ),
        scratch_shapes=[
            dma((2, slabs - 1)),
            dma((2, experts - 1, slabs)),
            dma((2, experts, slabs)),
            dma((2, slabs - 1)),
        ],
        compiler_params=pltpu.CompilerParams(
            collective_id=1, has_side_effects=True, vmem_limit_bytes=32 * MIB
        ),
        cost_estimate=cost(1e6, 16 * width * width),
        name="spread",
    )(w_query, w_key, w_value, w_out, extra)


def place_kernel(experts, cap, routes_ref, rank_col_ref, rank_row_ref, flat_ref, flat_t_ref):
    rows = routes_ref.shape[0]
    lane = iota((rows, LANES), 1)
    first, second = routes_ref[:, 0:1], routes_ref[:, 1:2]
    hot_first, hot_second = first == lane, second == lane
    hot = (hot_first.astype(F32) + hot_second.astype(F32)).astype(BF16)
    earlier = jnp.where(rank_row_ref[...] < rank_col_ref[...], 1.0, 0.0).astype(BF16)
    counts = dot(earlier, hot)

    def flat(hit, route):
        slot = jnp.sum(jnp.where(hit, counts, 0.0), axis=1, keepdims=True).astype(jnp.int32)
        return jnp.where((route < experts) & (slot < cap), route * cap + slot, experts * cap)

    out = jnp.where(
        lane == 0, flat(hot_first, first), jnp.where(lane == 1, flat(hot_second, second), 0)
    )
    flat_ref[...] = out
    flat_t_ref[...] = out.astype(F32).T[:8]


def place(routes, ranks, experts, cap):
    rows = routes.shape[0]
    return pl.pallas_call(
        functools.partial(place_kernel, experts, cap),
        out_shape=(
            jax.ShapeDtypeStruct((rows, LANES), jnp.int32),
            jax.ShapeDtypeStruct((8, rows), F32),
        ),
        compiler_params=params(32),
        cost_estimate=cost(2 * rows * rows * LANES, 8 * rows * LANES),
        name="place",
    )(routes, ranks.reshape(rows, 1), ranks.reshape(1, rows))


def qkv_kernel(ctx_ref, x_ref, extra_ref, w_ref, cos_ref, sin_ref, out_ref, aone_ref, whole_ref):
    half = x_ref.shape[1] // 2

    @pl.when(pl.program_id(0) == 0)
    def _():
        for which in range(3):
            whole_ref[which] = jnp.concatenate([w_ref[which, 0], w_ref[which, 1]], axis=1)

    values = x_ref[...].astype(F32)
    scale = lax.rsqrt(jnp.mean(values * values, axis=-1, keepdims=True) + EPS)
    normed = (values * scale * extra_ref[GAIN_ONE : GAIN_ONE + 1].astype(F32)).astype(BF16)
    aone_ref[...] = normed
    cos, sin = cos_ref[...], sin_ref[...]
    for which in range(3):
        product = dot(normed, whole_ref[which])
        for pair in range(2 * half // LANES):
            chunk = product[:, pair * LANES : (pair + 1) * LANES]
            if which < 2:
                chunk = chunk * cos + swap_halves(chunk) * sin
            if which == 0:
                chunk = chunk * HEAD_DIM ** (-0.5)
            side, place_in = pair // (half // LANES), pair % (half // LANES)
            out_ref[side, which, :, place_in * LANES : (place_in + 1) * LANES] = chunk.astype(BF16)


def project(ctx, x, extra, w_shared, cos, sin):
    rows, width = x.shape
    blocks = rows // TB
    return pl.pallas_call(
        qkv_kernel,
        grid_spec=pltpu.PrefetchScalarGridSpec(
            num_scalar_prefetch=1,
            grid=(blocks,),
            in_specs=[
                pl.BlockSpec((TB, width), lambda i, c: (i, 0)),
                pl.BlockSpec((LANES, width), lambda i, c: (0, 0)),
                pl.BlockSpec((3, 2, width, width // 2), lambda i, c: (0, 0, 0, 0)),
                pl.BlockSpec((TB, LANES), lambda i, c: (c[0] * blocks + i, 0)),
                pl.BlockSpec((TB, LANES), lambda i, c: (c[0] * blocks + i, 0)),
            ],
            out_specs=[
                pl.BlockSpec((2, 3, TB, width // 2), lambda i, c: (0, 0, i, 0)),
                pl.BlockSpec((TB, width), lambda i, c: (i, 0)),
            ],
            scratch_shapes=[pltpu.VMEM((3, width, width), BF16)],
        ),
        out_shape=(
            jax.ShapeDtypeStruct((2, 3, rows, width // 2), BF16),
            jax.ShapeDtypeStruct((rows, width), BF16),
        ),
        compiler_params=params(40),
        cost_estimate=cost(6 * rows * width * width, 6 * width * width + 12 * rows * width),
        name="project",
    )(ctx, x, extra, w_shared, cos, sin)


def head_masks():
    lane = iota((TQ, LANES), 1)
    low = jnp.where(lane < HEAD_DIM, 1.0, 0.0).astype(BF16)
    return low, (1.0 - low.astype(F32)).astype(BF16)


def attend_kernel(first_ref, q_ref, k_ref, v_ref, lo_ref, o_ref, lse_ref, vt_ref):
    per = q_ref.shape[2] // TQ
    count = 2 * per
    masks = head_masks()
    sub = iota((TQ, TQ), 0)
    diagonal = sub <= iota((TQ, TQ), 1)

    def turn(tile, carry):
        vt_ref[tile] = v_ref[tile // per, 0, pl.ds((tile % per) * TQ, TQ), :].T
        return carry

    lax.fori_loop(0, count, turn, 0)

    def q_step(qi, carry):
        rows = pl.ds((qi % per) * TQ, TQ)
        query = q_ref[qi // per, 0, rows, :]
        queries = [query * mask for mask in masks]
        low = lo_ref[qi]
        keys = k_ref[qi // per, 0, rows, :]
        turned = vt_ref[qi]
        ok = diagonal & (sub >= low - qi * TQ)
        state = []
        for head in range(2):
            scores = jnp.where(ok, dot_nt(keys, queries[head]), MASKED)
            peak = jnp.max(scores, axis=0, keepdims=True)
            probs = jnp.exp(scores - peak)
            total = jnp.sum(probs, axis=0, keepdims=True)
            mixed = dot(turned[head * HEAD_DIM : (head + 1) * HEAD_DIM], probs.astype(BF16))
            state += [peak, total, mixed]

        def k_step(ki, state):
            keys = k_ref[ki // per, 0, pl.ds((ki % per) * TQ, TQ), :]
            turned = vt_ref[ki]
            ok = sub >= low - ki * TQ
            new = []
            for head in range(2):
                peak, total, mixed = state[3 * head : 3 * head + 3]
                scores = jnp.where(ok, dot_nt(keys, queries[head]), MASKED)
                top = jnp.maximum(peak, jnp.max(scores, axis=0, keepdims=True))
                shrink = jnp.exp(peak - top)
                probs = jnp.exp(scores - top)
                total = total * shrink + jnp.sum(probs, axis=0, keepdims=True)
                part = dot(turned[head * HEAD_DIM : (head + 1) * HEAD_DIM], probs.astype(BF16))
                new += [top, total, mixed * shrink + part]
            return tuple(new)

        state = lax.fori_loop(first_ref[qi], qi, k_step, tuple(state))
        out = jnp.concatenate([state[2] / state[1], state[5] / state[4]], axis=0)
        o_ref[qi // per, rows, :] = out.T.astype(BF16)
        lse_ref[0, qi, 0:1, :] = state[0] + jnp.log(state[1])
        lse_ref[0, qi, 1:2, :] = state[3] + jnp.log(state[4])
        return carry

    lax.fori_loop(0, count, q_step, 0)


def part_spec(which, rows):
    return pl.BlockSpec((2, 1, rows, LANES), lambda p, first, which=which: (0, which, 0, p))


def attend(first, qkv, low):
    _, _, rows, half = qkv.shape
    pairs = half // LANES
    tiles = 2 * rows // TQ
    return pl.pallas_call(
        attend_kernel,
        grid_spec=pltpu.PrefetchScalarGridSpec(
            num_scalar_prefetch=1,
            grid=(pairs,),
            in_specs=[
                part_spec(0, rows),
                part_spec(1, rows),
                part_spec(2, rows),
                pl.BlockSpec((tiles, 1, TQ), lambda p, first: (0, 0, 0)),
            ],
            out_specs=[
                pl.BlockSpec((2, rows, LANES), lambda p, first: (0, 0, p)),
                pl.BlockSpec((1, tiles, 8, TQ), lambda p, first: (p, 0, 0, 0)),
            ],
            scratch_shapes=[pltpu.VMEM((tiles, LANES, TQ), BF16)],
        ),
        out_shape=(
            jax.ShapeDtypeStruct((2, rows, half), BF16),
            jax.ShapeDtypeStruct((pairs, tiles, 8, TQ), F32),
        ),
        compiler_params=params(40),
        cost_estimate=cost(40e9, 16 * rows * half, 12e6),
        name="attend",
    )(first, qkv, qkv, qkv, low)


def attend_back_kernel(
    first_ref,
    q_ref,
    k_ref,
    v_ref,
    do_ref,
    o_ref,
    lse_ref,
    lo_ref,
    cos_ref,
    sin_ref,
    g_ref,
    kt_ref,
    delta_ref,
    dk_ref,
    dv_ref,
):
    per = q_ref.shape[2] // TQ
    count = 2 * per
    masks = head_masks()
    sub = iota((TQ, TQ), 0)
    diagonal = sub <= iota((TQ, TQ), 1)

    def prepare(tile, carry):
        rows = pl.ds((tile % per) * TQ, TQ)
        kt_ref[tile] = k_ref[tile // per, 0, rows, :].T
        both = o_ref[tile // per, rows, :].astype(F32) * do_ref[tile // per, rows, :].astype(F32)
        both = both.T
        delta_ref[tile, 0:1, :] = jnp.sum(both[:HEAD_DIM], axis=0, keepdims=True)
        delta_ref[tile, 1:2, :] = jnp.sum(both[HEAD_DIM:], axis=0, keepdims=True)
        dk_ref[tile] = jnp.zeros((TQ, LANES), F32)
        dv_ref[tile] = jnp.zeros((TQ, LANES), F32)
        return carry

    lax.fori_loop(0, count, prepare, 0)

    def q_step(qi, carry):
        rows = pl.ds((qi % per) * TQ, TQ)
        query = q_ref[qi // per, 0, rows, :]
        grad = do_ref[qi // per, rows, :]
        queries = [query * mask for mask in masks]
        grads = [grad * mask for mask in masks]
        both_queries = jnp.concatenate(queries, axis=0)
        both_grads = jnp.concatenate(grads, axis=0)
        low = lo_ref[qi]
        lse = [lse_ref[0, qi, h : h + 1, :] for h in range(2)]
        delta = [delta_ref[qi, h : h + 1, :] for h in range(2)]

        def tile(ki, ok, sums):
            at = pl.ds((ki % per) * TQ, TQ)
            keys = k_ref[ki // per, 0, at, :]
            values = v_ref[ki // per, 0, at, :]
            turned = kt_ref[ki]
            all_probs, all_scores, new = [], [], []
            for h in range(2):
                scores = jnp.where(ok, dot_nt(keys, queries[h]), MASKED)
                probs = jnp.exp(scores - lse[h])
                grad_probs = dot_nt(values, grads[h])
                grad_scores = (probs * (grad_probs - delta[h])).astype(BF16)
                new.append(
                    sums[h] + dot(turned[h * HEAD_DIM : (h + 1) * HEAD_DIM], grad_scores)
                )
                all_probs.append(probs.astype(BF16))
                all_scores.append(grad_scores)
            dv_ref[ki] += dot(jnp.concatenate(all_probs, axis=1), both_grads)
            dk_ref[ki] += dot(jnp.concatenate(all_scores, axis=1), both_queries)
            return tuple(new)

        start = jnp.zeros((HEAD_DIM, TQ), F32)
        sums = tile(qi, diagonal & (sub >= low - qi * TQ), (start, start))
        sums = lax.fori_loop(
            first_ref[qi], qi, lambda ki, s: tile(ki, sub >= low - ki * TQ, s), sums
        )
        grad_query = jnp.concatenate(sums, axis=0).T * HEAD_DIM ** (-0.5)
        cos, sin = cos_ref[qi // per, rows, :], sin_ref[qi // per, rows, :]
        g_ref[qi // per, 0, rows, :] = (grad_query * cos - swap_halves(grad_query) * sin).astype(
            BF16
        )
        return carry

    lax.fori_loop(0, count, q_step, 0)

    def finish(tile, carry):
        rows = pl.ds((tile % per) * TQ, TQ)
        cos, sin = cos_ref[tile // per, rows, :], sin_ref[tile // per, rows, :]
        grad_key = dk_ref[tile]
        g_ref[tile // per, 1, rows, :] = (grad_key * cos - swap_halves(grad_key) * sin).astype(BF16)
        g_ref[tile // per, 2, rows, :] = dv_ref[tile].astype(BF16)
        return carry

    lax.fori_loop(0, count, finish, 0)


def attend_back(first, qkv, grad_o, o, lse, low, cos, sin):
    _, _, rows, half = qkv.shape
    pairs = half // LANES
    tiles = 2 * rows // TQ
    side = pl.BlockSpec((2, rows, LANES), lambda p, first: (0, 0, p))
    table = pl.BlockSpec((2, rows, LANES), lambda p, first: (0, 0, 0))
    return pl.pallas_call(
        attend_back_kernel,
        grid_spec=pltpu.PrefetchScalarGridSpec(
            num_scalar_prefetch=1,
            grid=(pairs,),
            in_specs=[
                part_spec(0, rows),
                part_spec(1, rows),
                part_spec(2, rows),
                side,
                side,
                pl.BlockSpec((1, tiles, 8, TQ), lambda p, first: (p, 0, 0, 0)),
                pl.BlockSpec((tiles, 1, TQ), lambda p, first: (0, 0, 0)),
                table,
                table,
            ],
            out_specs=pl.BlockSpec((2, 3, rows, LANES), lambda p, first: (0, 0, 0, p)),
            scratch_shapes=[
                pltpu.VMEM((tiles, LANES, TQ), BF16),
                pltpu.VMEM((tiles, 8, TQ), F32),
                pltpu.VMEM((tiles, TQ, LANES), F32),
                pltpu.VMEM((tiles, TQ, LANES), F32),
            ],
        ),
        out_shape=jax.ShapeDtypeStruct((2, 3, rows, half), BF16),
        compiler_params=params(48),
        cost_estimate=cost(100e9, 32 * rows * half, 12e6),
        name="attend_back",
    )(first, qkv, qkv, qkv, grad_o, o, lse, low, cos, sin)


def middle_kernel(
    total, x_ref, o_ref, w_ref, extra_ref, prev_ref, res_ref, routes_ref, hres_ref, atwo_ref, stat_ref
):
    attended = jnp.concatenate([o_ref[0], o_ref[1]], axis=1)
    hres = x_ref[...].astype(F32) + dot(
        attended, jnp.concatenate([w_ref[0, 0], w_ref[0, 1]], axis=1)
    )
    hres_ref[...] = hres
    scale = lax.rsqrt(jnp.mean(hres * hres, axis=-1, keepdims=True) + EPS)
    extra = extra_ref[...]
    gain = extra[GAIN_TWO : GAIN_TWO + 1].astype(F32)
    atwo = (hres * scale * gain).astype(BF16)
    atwo_ref[...] = atwo
    logits = dot_nt(atwo, extra)
    for j in range(total):
        logits = logits + prev_ref[:, j : j + 1] * res_ref[j : j + 1, :]
    lane = iota(logits.shape, 1)

    def soft(inside):
        peak = jnp.max(jnp.where(inside, logits, -jnp.inf), axis=1, keepdims=True)
        powers = jnp.where(inside, jnp.exp(jnp.where(inside, logits - peak, 0.0)), 0.0)
        return powers / jnp.sum(powers, axis=1, keepdims=True)

    probs = soft(lane < total)
    stat = probs
    for j in range(2):
        start = total + 2 * j
        stat = stat + soft((lane >= start) & (lane < start + 2))
    stat = jnp.where(lane == total + 4, scale, stat)
    for k in range(2):
        gate = jnp.sum(
            jnp.where(lane == routes_ref[:, k : k + 1], probs, 0.0), axis=1, keepdims=True
        )
        stat = jnp.where(lane == total + 5 + k, gate, stat)
    stat_ref[...] = stat


def middle(total, x, o, w_shared, extra, prev, res, routes):
    rows, width = x.shape
    token = lambda i: (i, 0)
    whole = lambda i: (0, 0)
    return pl.pallas_call(
        functools.partial(middle_kernel, total),
        grid=(rows // TB,),
        in_specs=[
            pl.BlockSpec((TB, width), token),
            pl.BlockSpec((2, TB, width // 2), lambda i: (0, i, 0)),
            pl.BlockSpec((1, 2, width, width // 2), lambda i: (3, 0, 0, 0)),
            pl.BlockSpec((LANES, width), whole),
            pl.BlockSpec((TB, total), token),
            pl.BlockSpec((total, LANES), whole),
            pl.BlockSpec((TB, 2), token),
        ],
        out_specs=[
            pl.BlockSpec((TB, width), token),
            pl.BlockSpec((TB, width), token),
            pl.BlockSpec((TB, LANES), token),
        ],
        out_shape=(
            jax.ShapeDtypeStruct((rows, width), F32),
            jax.ShapeDtypeStruct((rows, width), BF16),
            jax.ShapeDtypeStruct((rows, LANES), F32),
        ),
        compiler_params=params(40),
        cost_estimate=cost(2 * rows * width * width, 2 * width * width + 10 * rows * width),
        name="middle",
    )(x, o, w_shared, extra, prev, res, routes)


def expert_kernel(
    total,
    flat_ref,
    atwo_ref,
    dy_ref,
    stat_ref,
    wg_ref,
    wu_ref,
    wd_ref,
    flow_ref,
    drow_ref,
    gg_ref,
    gu_ref,
    gd_ref,
    send_x,
    send_g,
    all_x,
    all_g,
    acc_ref,
    z_ref,
    a_ref,
    b_ref,
    turned_ref,
    wide_buf,
    down_buf,
    wide_given,
    wide_taken,
    down_given,
    down_taken,
    x_sems,
    g_sems,
    flow_sems,
    drow_sems,
    local_sems,
    weight_sems,
    wide_sems,
    down_sems,
):
    experts, cap, width = all_x.shape
    slots = experts * cap
    chunks = z_ref.shape[0]
    per = chunks // 2
    half = width // 2
    tokens = atwo_ref.shape[0]
    me, core = lax.axis_index("expert"), lax.axis_index("context")

    def weights(step):
        chunk, slot = lax.rem(step, chunks), lax.rem(step, 2)
        at = pl.ds(pl.multiple_of(lax.rem(chunk, per) * FC, FC), FC)
        rows = pl.ds(pl.multiple_of(chunk * FC, FC), FC)
        return (
            pltpu.make_async_copy(
                wg_ref.at[chunk // per, :, at], wide_buf.at[slot, 0], weight_sems.at[slot, 0]
            ),
            pltpu.make_async_copy(
                wu_ref.at[chunk // per, :, at], wide_buf.at[slot, 1], weight_sems.at[slot, 1]
            ),
            pltpu.make_async_copy(
                wd_ref.at[0, rows, :], down_buf.at[slot, 0], weight_sems.at[slot, 2]
            ),
            pltpu.make_async_copy(
                wd_ref.at[1, rows, :], down_buf.at[slot, 1], weight_sems.at[slot, 3]
            ),
        )

    def next_weights(step):
        @pl.when(step + 1 < 2 * chunks)
        def _():
            for copy in weights(step + 1):
                copy.start()

        for copy in weights(step):
            copy.wait()

    for copy in weights(0):
        copy.start()
    greet_all(("context", "expert"))

    def hots(target):
        slot = (iota((cap, tokens), 0) + target * cap).astype(F32)
        return flat_ref[0:1, :] == slot, flat_ref[1:2, :] == slot

    order = list(range(1, experts)) + [0]
    x_copies, g_copies = {}, {}
    for j in order:
        target = lax.rem(me + j, experts)
        first, second = hots(target)
        rows = dot(jnp.where(first | second, 1.0, 0.0).astype(BF16), atwo_ref[...]).astype(BF16)
        if j == 0:
            all_x[0] = rows
        else:
            send_x[j - 1] = rows
            x_copies[j] = remote(
                send_x.at[j - 1], all_x.at[j], x_sems, (j - 1,), {"expert": target}
            )
            x_copies[j].start()
    gates = stat_ref[...].T
    for j in order:
        target = lax.rem(me + j, experts)
        first, second = hots(target)
        gate = jnp.sum(
            jnp.where(first, gates[total + 5 : total + 6], 0.0)
            + jnp.where(second, gates[total + 6 : total + 7], 0.0),
            axis=1,
            keepdims=True,
        )
        rows = dot(jnp.where(first | second, 1.0, 0.0).astype(BF16), dy_ref[...])
        rows = (rows * gate).astype(BF16)
        if j == 0:
            all_g[0] = rows
        else:
            send_g[j - 1] = rows
            g_copies[j] = remote(
                send_g.at[j - 1], all_g.at[j], g_sems, (j - 1,), {"expert": target}
            )
            g_copies[j].start()

    def back(buffer, dest, sems, j):
        return remote(
            buffer.at[j - 1],
            dest.at[me],
            sems,
            (j - 1,),
            {"expert": lax.rem(me + experts - j, experts)},
        )

    for j in range(1, experts):
        x_copies[j].wait()
    acc_ref[...] = jnp.zeros_like(acc_ref)

    def up(step, carry):
        next_weights(step)
        slot = lax.rem(step, 2)
        rows = all_x[...].reshape(slots, width)
        gate = dot(rows, wide_buf[slot, 0])
        lift = dot(rows, wide_buf[slot, 1])
        sig = 1.0 / (1.0 + jnp.exp(-gate))
        swish = gate * sig
        hidden = (swish * lift).astype(BF16)
        z_ref[step] = hidden
        a_ref[step] = (lift * sig * (1.0 + gate * (1.0 - sig))).astype(BF16)
        b_ref[step] = swish.astype(BF16)
        acc_ref[...] += dot(hidden, jnp.concatenate([down_buf[slot, 0], down_buf[slot, 1]], axis=1))
        return carry

    lax.fori_loop(0, chunks, up, 0)
    own = [
        pltpu.make_async_copy(all_own, dest.at[me], local_sems.at[i])
        for i, (all_own, dest) in enumerate(
            ((send_x.at[experts - 1], flow_ref), (send_g.at[experts - 1], drow_ref))
        )
    ]
    for j in range(1, experts):
        send_x[j - 1] = acc_ref[j * cap : (j + 1) * cap, :].astype(BF16)
        back(send_x, flow_ref, flow_sems, j).start()
    send_x[experts - 1] = acc_ref[:cap, :].astype(BF16)
    own[0].start()
    turned_ref[...] = all_x[...].reshape(slots, width).T
    acc_ref[...] = jnp.zeros_like(acc_ref)
    for j in range(1, experts):
        g_copies[j].wait()

    def down(step, carry):
        next_weights(step + chunks)
        slot = lax.rem(step, 2)
        whole = jnp.concatenate([down_buf[slot, 0], down_buf[slot, 1]], axis=1)
        dz = dot_nt(all_g[...].reshape(slots, width), whole)
        dg = (dz * a_ref[step].astype(F32)).astype(BF16)
        du = (dz * b_ref[step].astype(F32)).astype(BF16)
        a_ref[step] = dg
        b_ref[step] = du
        acc_ref[...] += dot_nt(dg, wide_buf[slot, 0]) + dot_nt(du, wide_buf[slot, 1])
        return carry

    lax.fori_loop(0, chunks, down, 0)
    for j in range(1, experts):
        send_g[j - 1] = acc_ref[j * cap : (j + 1) * cap, :].astype(BF16)
        back(send_g, drow_ref, drow_sems, j).start()
    send_g[experts - 1] = acc_ref[:cap, :].astype(BF16)
    own[1].start()

    def wide_copy(step):
        return remote(
            wide_given.at[step],
            wide_taken.at[step],
            wide_sems,
            (step,),
            {"context": 1 - core},
        )

    def down_copy(step):
        chunk = lax.rem((1 - core) * per + step, chunks)
        return remote(
            down_given.at[step],
            down_taken.at[chunk],
            down_sems,
            (chunk,),
            {"context": 1 - core},
        )

    def products(step):
        chunk = lax.rem((1 - core) * per + step, chunks)
        gate = dot(turned_ref[...], a_ref[chunk])
        lift = dot(turned_ref[...], b_ref[chunk])
        low = dot(z_ref[chunk].T, all_g[...].reshape(slots, width))
        left, right = low[:, :half], low[:, half:]
        down_given[step] = jnp.where(core == 0, right, left).astype(BF16)
        gd_ref[chunk] = jnp.where(core == 0, left, right).astype(BF16)
        down_copy(step).start()
        return gate, lift

    def give(step, carry):
        gate, lift = products(step)
        wide_given[step, 0] = gate.astype(BF16)
        wide_given[step, 1] = lift.astype(BF16)
        wide_copy(step).start()
        return carry

    lax.fori_loop(0, per, give, 0)

    def keep(step, carry):
        gate, lift = products(step)
        wide_copy(step - per).wait_recv()
        gg_ref[step - per] = (gate + wide_taken[step - per, 0].astype(F32)).astype(BF16)
        gu_ref[step - per] = (lift + wide_taken[step - per, 1].astype(F32)).astype(BF16)
        return carry

    lax.fori_loop(per, chunks, keep, 0)

    def settle(step, carry):
        other = lax.rem(core * per + step, chunks)
        copy = remote(
            down_given.at[step],
            down_taken.at[other],
            down_sems,
            (other,),
            {"context": 1 - core},
        )
        copy.wait_recv()
        gd_ref[other] = (gd_ref[other].astype(F32) + down_taken[other].astype(F32)).astype(BF16)
        return carry

    lax.fori_loop(0, chunks, settle, 0)

    for copy in own:
        copy.wait()
    for j in range(1, experts):
        back(send_x, flow_ref, flow_sems, j).wait()
        back(send_g, drow_ref, drow_sems, j).wait()

    def sent(step, carry):
        down_copy(step).wait_send()
        return carry

    lax.fori_loop(0, chunks, sent, 0)
    lax.fori_loop(0, per, lambda step, carry: (wide_copy(step).wait_send(), carry)[1], 0)


def run_experts(total, experts, cap, flat_t, atwo, dy, stat, wg, wu, wd):
    rows, width = atwo.shape
    hidden = wd.shape[1]
    chunks = hidden // FC
    per = chunks // 2
    half = width // 2
    slots = experts * cap
    vmem = pl.BlockSpec(memory_space=pltpu.VMEM)
    anywhere = pl.BlockSpec(memory_space=pl.ANY)
    dma = pltpu.SemaphoreType.DMA
    return pl.pallas_call(
        functools.partial(expert_kernel, total),
        in_specs=[vmem] * 4 + [anywhere] * 3,
        out_specs=[anywhere] * 2 + [vmem] * 3,
        out_shape=(
            jax.ShapeDtypeStruct((experts, cap, width), BF16),
            jax.ShapeDtypeStruct((experts, cap, width), BF16),
            jax.ShapeDtypeStruct((per, width, FC), BF16),
            jax.ShapeDtypeStruct((per, width, FC), BF16),
            jax.ShapeDtypeStruct((chunks, FC, half), BF16),
        ),
        scratch_shapes=[
            pltpu.VMEM((experts, cap, width), BF16),
            pltpu.VMEM((experts, cap, width), BF16),
            pltpu.VMEM((experts, cap, width), BF16),
            pltpu.VMEM((experts, cap, width), BF16),
            pltpu.VMEM((slots, width), F32),
            pltpu.VMEM((chunks, slots, FC), BF16),
            pltpu.VMEM((chunks, slots, FC), BF16),
            pltpu.VMEM((chunks, slots, FC), BF16),
            pltpu.VMEM((width, slots), BF16),
            pltpu.VMEM((2, 2, width, FC), BF16),
            pltpu.VMEM((2, 2, FC, half), BF16),
            pltpu.VMEM((per, 2, width, FC), BF16),
            pltpu.VMEM((per, 2, width, FC), BF16),
            pltpu.VMEM((chunks, FC, half), BF16),
            pltpu.VMEM((chunks, FC, half), BF16),
            dma((2, experts - 1)),
            dma((2, experts - 1)),
            dma((2, experts - 1)),
            dma((2, experts - 1)),
            dma((2,)),
            dma((2, 4)),
            dma((2, per)),
            dma((2, chunks)),
        ],
        compiler_params=pltpu.CompilerParams(
            collective_id=2, has_side_effects=True, vmem_limit_bytes=62 * MIB
        ),
        cost_estimate=cost(18 * slots * width * hidden, 30 * width * hidden),
        name="experts",
    )(flat_t, atwo, dy, stat, wg, wu, wd)


def combine_kernel(
    experts,
    total,
    flow_ref,
    drow_ref,
    flat_ref,
    stat_ref,
    routes_ref,
    hres_ref,
    atwo_ref,
    dy_ref,
    o_ref,
    extra_ref,
    w_ref,
    prev_ref,
    out_ref,
    dh_ref,
    dolow_ref,
    gw_ref,
    small_ref,
    acc_ref,
):
    step = pl.program_id(0)
    slots = flow_ref.shape[0]
    half = o_ref.shape[2]
    extra = extra_ref[...]
    gain = extra[GAIN_TWO : GAIN_TWO + 1].astype(F32)
    stat = stat_ref[...]
    hres = hres_ref[...]
    dy = dy_ref[...].astype(F32)
    scale = stat[:, total + 4 : total + 5]
    gates = [stat[:, total + 5 + k : total + 6 + k] for k in range(2)]
    ntwo = hres * scale * gain
    spread = iota((TB, slots), 1)
    hots = [flat_ref[:, k : k + 1] == spread for k in range(2)]
    returned = flow_ref[...]
    mixes = [[stat[:, total + 2 * j + i : total + 2 * j + i + 1] for i in range(2)] for j in range(2)]
    vecs = [extra[VECS + j : VECS + j + 1].astype(F32) for j in range(2)]
    moe = jnp.zeros_like(hres)
    lane = iota((TB, LANES), 1)
    dpgate = jnp.zeros((TB, LANES), F32)
    weight = jnp.zeros((TB, 1), F32)
    const_weights = [jnp.zeros((TB, 1), F32)] * 2
    for k in range(2):
        route = routes_ref[:, k : k + 1]
        epair = dot(jnp.where(hots[k], 1.0, 0.0).astype(BF16), returned)
        share = jnp.where(route == experts + 1, 1.0, 0.0)
        weight = weight + share * gates[k]
        for j in range(2):
            chosen = jnp.where(route == experts + 2 + j, 1.0, 0.0)
            share = share + chosen * mixes[j][0]
            epair = epair + (chosen * mixes[j][1]) * vecs[j]
            const_weights[j] = const_weights[j] + chosen * gates[k]
        epair = epair + share * ntwo
        moe = moe + gates[k] * epair
        dgate = jnp.sum(dy * epair, axis=1, keepdims=True)
        dpgate = dpgate + jnp.where(lane == route, dgate, 0.0)
    out_ref[...] = (hres + moe).astype(BF16)

    pgate = jnp.where(lane < total, stat, 0.0)
    dlogit = pgate * (dpgate - jnp.sum(pgate * dpgate, axis=1, keepdims=True))
    dot_normed = jnp.sum(dy * ntwo, axis=1, keepdims=True)
    droute = dlogit
    vec_rows = []
    for j in range(2):
        dot_vec = jnp.sum(dy * vecs[j], axis=1, keepdims=True)
        grads = [const_weights[j] * dot_normed, const_weights[j] * dot_vec]
        inner = mixes[j][0] * grads[0] + mixes[j][1] * grads[1]
        for i in range(2):
            droute = jnp.where(
                lane == total + 2 * j + i, mixes[j][i] * (grads[i] - inner), droute
            )
        weight = weight + const_weights[j] * mixes[j][0]
        vec_rows.append(jnp.sum((const_weights[j] * mixes[j][1]) * dy, axis=0, keepdims=True))
    droute = droute.astype(BF16)
    hot_any = jnp.where(hots[0] | hots[1], 1.0, 0.0).astype(BF16)
    dntwo = weight * dy + dot(droute, extra) + dot(hot_any, drow_ref[...])
    turned = dntwo * gain
    inner = jnp.mean(hres * turned, axis=1, keepdims=True)
    dh = dy + scale * turned - hres * (scale * scale * scale * inner)
    dh_ref[...] = dh
    dhlow = dh.astype(BF16)
    w_out = jnp.concatenate([w_ref[0, 0], w_ref[0, 1]], axis=1)
    dolow = dot_nt(dhlow, w_out).astype(BF16)
    dolow_ref[0] = dolow[:, :half]
    dolow_ref[1] = dolow[:, half:]
    gain_row = jnp.sum(dntwo * hres * scale, axis=0, keepdims=True)
    route_rows = dot(droute.T, atwo_ref[...])
    res_rows = lax.dot_general(
        prev_ref[...],
        dlogit,
        (((0,), (0,)), ((), ())),
        precision=HIGH,
        preferred_element_type=F32,
    )
    width = hres.shape[1]
    res_rows = jnp.concatenate([res_rows, jnp.zeros((total, width - LANES), F32)], axis=1)
    small = jnp.concatenate(
        [route_rows[: total + 4], gain_row, vec_rows[0], vec_rows[1], jnp.zeros((1, width), F32), res_rows],
        axis=0,
    )
    part = dot(jnp.concatenate([o_ref[0], o_ref[1]], axis=1).T, dhlow)

    @pl.when(step == 0)
    def _():
        small_ref[...] = small
        acc_ref[...] = part

    @pl.when(step > 0)
    def _():
        small_ref[...] += small
        acc_ref[...] += part

    @pl.when(step == pl.num_programs(0) - 1)
    def _():
        for side in range(2):
            gw_ref[side] = acc_ref[:, side * half : (side + 1) * half].astype(BF16)


def combine(experts, total, flow, drow, flat, stat, routes, hres, atwo, dy, o, w_shared, extra, prev):
    rows, width = hres.shape
    slots = flow.shape[0]
    half = width // 2
    token = lambda i: (i, 0)
    whole = lambda i: (0, 0)
    side = pl.BlockSpec((2, TB, half), lambda i: (0, i, 0))
    weight = pl.BlockSpec((2, width, half), lambda i: (0, 0, 0))
    small_rows = 2 * total + 8
    return pl.pallas_call(
        functools.partial(combine_kernel, experts, total),
        grid=(rows // TB,),
        in_specs=[
            pl.BlockSpec((slots, width), whole),
            pl.BlockSpec((slots, width), whole),
            pl.BlockSpec((TB, LANES), token),
            pl.BlockSpec((TB, LANES), token),
            pl.BlockSpec((TB, 2), token),
            pl.BlockSpec((TB, width), token),
            pl.BlockSpec((TB, width), token),
            pl.BlockSpec((TB, width), token),
            side,
            pl.BlockSpec((LANES, width), whole),
            pl.BlockSpec((1, 2, width, half), lambda i: (3, 0, 0, 0)),
            pl.BlockSpec((TB, total), token),
        ],
        out_specs=[
            pl.BlockSpec((TB, width), token),
            pl.BlockSpec((TB, width), token),
            side,
            weight,
            pl.BlockSpec((small_rows, width), whole),
        ],
        out_shape=(
            jax.ShapeDtypeStruct((rows, width), BF16),
            jax.ShapeDtypeStruct((rows, width), F32),
            jax.ShapeDtypeStruct((2, rows, half), BF16),
            jax.ShapeDtypeStruct((2, width, half), BF16),
            jax.ShapeDtypeStruct((small_rows, width), F32),
        ),
        scratch_shapes=[pltpu.VMEM((width, width), F32)],
        compiler_params=params(56),
        cost_estimate=cost(
            6 * rows * slots * width + 4 * rows * width * width, 30 * rows * width + 8 * width * width
        ),
        name="combine",
    )(flow, drow, flat, stat, routes, hres, atwo, dy, o, extra, w_shared, prev)


def project_back_kernel(
    g_ref, w_ref, extra_ref, x_ref, aone_ref, dh_ref, gwo_ref, out_ref, gw_ref, gain_out_ref, acc_ref
):
    step = pl.program_id(0)
    half = g_ref.shape[3]
    turned = aone_ref[...].T
    dnone = None
    for which in range(3):
        grad = jnp.concatenate([g_ref[0, which], g_ref[1, which]], axis=1)
        part = dot_nt(grad, jnp.concatenate([w_ref[which, 0], w_ref[which, 1]], axis=1))
        dnone = part if dnone is None else dnone + part
        weight = dot(turned, grad)

        @pl.when(step == 0)
        def _():
            acc_ref[which] = weight

        @pl.when(step > 0)
        def _():
            acc_ref[which] += weight

    values = x_ref[...].astype(F32)
    scale = lax.rsqrt(jnp.mean(values * values, axis=-1, keepdims=True) + EPS)
    scaled = dnone * extra_ref[GAIN_ONE : GAIN_ONE + 1].astype(F32)
    inner = jnp.mean(values * scaled, axis=1, keepdims=True)
    out_ref[...] = dh_ref[...] + scale * scaled - values * (scale * scale * scale * inner)
    row = jnp.sum(dnone * values * scale, axis=0, keepdims=True)

    @pl.when(step == 0)
    def _():
        gain_out_ref[...] = row

    @pl.when(step > 0)
    def _():
        gain_out_ref[...] += row

    @pl.when(step == pl.num_programs(0) - 1)
    def _():
        for side in range(2):
            for which in range(3):
                at = side * half
                gw_ref[side, which] = acc_ref[which, :, at : at + half].astype(BF16)
            gw_ref[side, 3] = gwo_ref[side]


def project_back(grad, w_shared, extra, x, aone, dh, grad_out_w):
    rows, width = x.shape
    half = width // 2
    token = lambda i: (i, 0)
    whole = lambda i: (0, 0)
    return pl.pallas_call(
        project_back_kernel,
        grid=(rows // TB,),
        in_specs=[
            pl.BlockSpec((2, 3, TB, half), lambda i: (0, 0, i, 0)),
            pl.BlockSpec((3, 2, width, half), lambda i: (0, 0, 0, 0)),
            pl.BlockSpec((LANES, width), whole),
            pl.BlockSpec((TB, width), token),
            pl.BlockSpec((TB, width), token),
            pl.BlockSpec((TB, width), token),
            pl.BlockSpec((2, width, half), lambda i: (0, 0, 0)),
        ],
        out_specs=[
            pl.BlockSpec((TB, width), token),
            pl.BlockSpec((2, 4, width, half), lambda i: (0, 0, 0, 0)),
            pl.BlockSpec((1, width), whole),
        ],
        out_shape=(
            jax.ShapeDtypeStruct((rows, width), F32),
            jax.ShapeDtypeStruct((2, 4, width, half), BF16),
            jax.ShapeDtypeStruct((1, width), F32),
        ),
        scratch_shapes=[pltpu.VMEM((3, width, width), F32)],
        compiler_params=params(56),
        cost_estimate=cost(12 * rows * width * width, 18 * width * width + 20 * rows * width),
        name="project_back",
    )(grad, w_shared, extra, x, aone, dh, grad_out_w)


def reduce_kernel(
    gain_at,
    grads_ref,
    small_ref,
    gain_ref,
    out_ref,
    small_out_ref,
    core_in,
    plane_out,
    plane_in,
    slab_out,
    slab_in,
    final,
    own_ref,
    small_own,
    small_core,
    small_plane,
    small_slab,
    core_sems,
    plane_sems,
    slab_sems,
    final_sems,
    pass_sems,
    small_core_sems,
    small_plane_sems,
    small_slab_sems,
):
    experts = lax.axis_size("expert")
    slabs = lax.axis_size("dp")
    me, core, slab = lax.axis_index("expert"), lax.axis_index("context"), lax.axis_index("dp")
    other = 1 - core

    greet_all(("context", "expert", "dp"))
    send = remote

    order = list(range(1, experts)) + [0]
    core_copies = {}
    for j in order:
        core_copies[j] = send(
            grads_ref.at[other, lax.rem(me + j, experts)],
            core_in.at[j],
            core_sems,
            (j,),
            {"context": other},
        )
        core_copies[j].start()
    row = iota(small_ref.shape, 0)
    small_own[...] = small_ref[...] + jnp.where(row == gain_at, gain_ref[...], 0.0)
    small_copy = send(small_own, small_core, small_core_sems, (0,), {"context": other})
    small_copy.start()

    def plane_copy(j, at):
        return send(
            plane_out.at[j - 1, at],
            plane_in.at[j - 1, at],
            plane_sems,
            (j - 1, at),
            {"expert": lax.rem(me + j, experts)},
        )

    for j in range(1, experts):
        core_copies[j].wait_recv()
        which = lax.rem(me + j, experts)

        def pass_on(k, j=j, which=which):
            at = lax.rem(slab + k + 1, slabs)
            plane_out[j - 1, at] = (
                grads_ref[core, which, at].astype(F32) + core_in[j, at].astype(F32)
            ).astype(BF16)
            plane_copy(j, at).start()

        loop(slabs, pass_on)
    core_copies[0].wait_recv()

    small_copy.wait()
    small_plane[me] = small_own[...] + small_core[...]
    small_plane_copies = []
    for j in range(1, experts):
        small_plane_copies.append(
            send(
                small_plane.at[me],
                small_plane.at[me],
                small_plane_sems,
                (j,),
                {"expert": lax.rem(me + j, experts)},
            )
        )
        small_plane_copies[-1].start()

    def gathered(at):
        value = grads_ref[core, me, at].astype(F32) + core_in[0, at].astype(F32)
        for j in range(1, experts):
            plane_copy(j, at).wait_recv()
            value = value + plane_in[j - 1, at].astype(F32)
        return value

    def slab_copy(k):
        return send(
            slab_out.at[k],
            slab_in.at[k],
            slab_sems,
            (k,),
            {"dp": lax.rem(slab + k + 1, slabs)},
        )

    def scatter(k):
        slab_out[k] = gathered(lax.rem(slab + k + 1, slabs)).astype(BF16)
        slab_copy(k).start()

    loop(slabs - 1, scatter)

    for copy in small_plane_copies:
        copy.wait()
    value = small_plane[0]
    for j in range(1, experts):
        value = value + small_plane[j]
    small_slab[slab] = value

    def small_slab_copy(k):
        return send(
            small_slab.at[slab],
            small_slab.at[slab],
            small_slab_sems,
            (k,),
            {"dp": lax.rem(slab + k + 1, slabs)},
        )

    loop(slabs - 1, lambda k: small_slab_copy(k).start())

    own_ref[...] = gathered(slab)

    def collect(k):
        slab_copy(k).wait_recv()
        own_ref[...] += slab_in[k].astype(F32)

    loop(slabs - 1, collect)
    final[core, me] = own_ref[...].astype(BF16)
    final_copies, pass_copies = [], []
    for j in range(1, experts):
        final_copies.append(
            send(
                final.at[core, me],
                final.at[core, me],
                final_sems,
                (j,),
                {"expert": lax.rem(me + j, experts)},
            )
        )
        final_copies[-1].start()
    for j in range(experts):
        source = lax.rem(me + experts - j, experts)
        if j > 0:
            final_copies[j - 1].wait_recv()
        pass_copies.append(
            send(
                final.at[core, source],
                final.at[core, source],
                pass_sems,
                (j,),
                {"context": other},
            )
        )
        pass_copies[-1].start()

    loop(slabs - 1, lambda k: small_slab_copy(k).wait())
    small_out_ref[...] = small_slab[0]

    def add_small(k):
        small_out_ref[...] += small_slab[k + 1]

    loop(slabs - 1, add_small)

    for copy in pass_copies:
        copy.wait_recv()
    half = final.shape[3]
    for which in range(experts):
        for side in range(2):
            out_ref[which, :, side * half : (side + 1) * half] = final[side, which].astype(F32)

    for j in range(experts):
        core_copies[j].wait_send()
    for j in range(1, experts):

        def sent(k, j=j):
            plane_copy(j, k).wait_send()

        loop(slabs, sent)
    loop(slabs - 1, lambda k: slab_copy(k).wait_send())
    for copy in final_copies + pass_copies:
        copy.wait_send()


def reduce_shared(mesh_sizes, grads, small, gain_row, gain_at):
    experts, slabs = mesh_sizes
    _, _, _, rows, half = grads.shape
    small_shape = small.shape
    vmem = pl.BlockSpec(memory_space=pltpu.VMEM)
    dma = pltpu.SemaphoreType.DMA
    return pl.pallas_call(
        functools.partial(reduce_kernel, gain_at),
        in_specs=[vmem] * 3,
        out_specs=[vmem] * 2,
        out_shape=(
            jax.ShapeDtypeStruct((experts, rows, 2 * half), F32),
            jax.ShapeDtypeStruct(small_shape, F32),
        ),
        scratch_shapes=[
            pltpu.VMEM((experts, slabs, rows, half), BF16),
            pltpu.VMEM((experts - 1, slabs, rows, half), BF16),
            pltpu.VMEM((experts - 1, slabs, rows, half), BF16),
            pltpu.VMEM((slabs - 1, rows, half), BF16),
            pltpu.VMEM((slabs - 1, rows, half), BF16),
            pltpu.VMEM((2, experts, rows, half), BF16),
            pltpu.VMEM((rows, half), F32),
            pltpu.VMEM(small_shape, F32),
            pltpu.VMEM(small_shape, F32),
            pltpu.VMEM((experts,) + small_shape, F32),
            pltpu.VMEM((slabs,) + small_shape, F32),
            dma((2, experts)),
            dma((2, experts - 1, slabs)),
            dma((2, slabs - 1)),
            dma((2, experts)),
            dma((2, experts)),
            dma((2, 1)),
            dma((2, experts)),
            dma((2, slabs - 1)),
        ],
        compiler_params=pltpu.CompilerParams(
            collective_id=0, has_side_effects=True, vmem_limit_bytes=56 * MIB
        ),
        cost_estimate=cost(1e6, 2 * grads.size),
        name="reduce_shared",
    )(grads, small, gain_row)


def swap_cores(value):
    return lax.all_to_all(value, "context", split_axis=0, concat_axis=0, tiled=True)


def on_device(
    tokens,
    segments,
    routes,
    prev_logits,
    ranks,
    cotangent,
    norm_one,
    w_query,
    w_key,
    w_value,
    w_out,
    norm_two,
    router,
    w_res,
    const_mix,
    const_vec,
    w_gate,
    w_up,
    w_down,
):
    experts = lax.axis_size("expert")
    dp = lax.axis_size("dp")
    total = experts + NZ
    _, rows, width = tokens.shape
    hidden = w_gate.shape[2]
    cap = (18 * rows + 8 * total - 1) // (8 * total)
    seq = 2 * rows
    tiles = seq // TQ
    core = lax.axis_index("context")
    half = width // 2

    def mine(shard, size):
        return lax.dynamic_slice_in_dim(shard, core * size, size, 1)

    def gather(shard):
        return lax.all_gather(shard, ("context", "dp"), axis=0).reshape(
            2, dp * shard.shape[0], shard.shape[1]
        )

    extra = jnp.concatenate(
        [router, const_mix, norm_one[:, None], norm_two[:, None], const_vec], axis=1
    )
    w_shared, extra = spread(experts, dp, w_query, w_key, w_value, w_out, extra.astype(F32).T)
    w_shared = w_shared.reshape(4, 2, width, half)
    extra = extra.transpose(1, 0, 2).reshape(total + 8, width).astype(BF16)
    extra = jnp.concatenate(
        [
            extra[: total + 4],
            jnp.zeros((GAIN_ONE - total - 4, width), BF16),
            extra[total + 4 :],
            jnp.zeros((LANES - GAIN_ONE - 4, width), BF16),
        ],
        axis=0,
    )
    gate_w = gather(mine(w_gate[0], hidden // 2))
    up_w = gather(mine(w_up[0], hidden // 2))
    down_w = gather(mine(w_down[0], half))

    flat, flat_t = place(routes[0], ranks[0, 0], experts, cap)
    segs = lax.all_gather(segments[0], "context", axis=0, tiled=True)
    places = jnp.arange(seq, dtype=jnp.int32)
    starts = jnp.sum((segs[None, :] < segs[:, None]).astype(jnp.int32), axis=1)
    low = jnp.maximum(starts, places - (WIN - 1)).reshape(tiles, 1, TQ)
    first = low[:, 0, 0] // TQ
    cos, sin = rope_tables(seq)
    cos, sin = jnp.asarray(cos), jnp.asarray(sin)
    res = jnp.pad(w_res.astype(F32), ((0, 0), (0, LANES - total)))

    x = tokens[0]
    dy = cotangent[0]
    sent, aone = project(core.reshape(1), x, extra, w_shared, cos, sin)
    qkv = swap_cores(sent)
    o_heads, lse = attend(first, qkv, low)
    o = swap_cores(o_heads)
    hres, atwo, stat = middle(total, x, o, w_shared, extra, prev_logits[0], res, routes[0])
    flow_back, drow_back, grad_gate, grad_up, grad_down = run_experts(
        total, experts, cap, flat_t, atwo, dy, stat, gate_w, up_w, down_w
    )
    flow_back = flow_back.reshape(experts * cap, width)
    drow_back = drow_back.reshape(experts * cap, width)

    def scatter_half(chip):
        share = lax.psum_scatter(chip, "dp", scatter_dimension=0, tiled=True)
        both = lax.all_gather(share, "context", axis=1, tiled=True)
        return both.astype(F32)[None]

    def columns(grad):
        return grad.transpose(1, 0, 2).reshape(width, hidden // 2)

    total_gate, total_up, total_down = (
        scatter_half(columns(grad_gate)),
        scatter_half(columns(grad_up)),
        scatter_half(grad_down.reshape(hidden, half)),
    )

    output, dh, dolow, grad_out_w, small = combine(
        experts,
        total,
        flow_back,
        drow_back,
        flat,
        stat,
        routes[0],
        hres,
        atwo,
        dy,
        o,
        w_shared,
        extra,
        prev_logits[0],
    )
    grad_o = swap_cores(dolow)
    grads_sent = attend_back(
        first,
        qkv,
        grad_o,
        o_heads,
        lse,
        low,
        cos.reshape(2, rows, LANES),
        sin.reshape(2, rows, LANES),
    )
    grads = swap_cores(grads_sent)
    grad_tokens, grad_shared, gain_row = project_back(grads, w_shared, extra, x, aone, dh, grad_out_w)
    shared, small = reduce_shared(
        (experts, dp),
        grad_shared.reshape(2, 4, dp, width // dp, half),
        small,
        gain_row,
        total + 7,
    )
    part = width // dp
    owned = lax.dynamic_slice_in_dim(small, lax.axis_index("dp") * part, part, 1)
    grad_res_total = small[total + 8 :, :total]
    return (
        output[None],
        grad_tokens[None],
        owned[total + 7],
        shared[0],
        shared[1],
        shared[2],
        shared[3],
        owned[total + 4],
        owned[:total].T,
        grad_res_total,
        owned[total : total + 4].T,
        owned[total + 5 : total + 7].T,
        total_gate,
        total_up,
        total_down,
    )


def solution(mesh):
    token = P(("expert", "dp"), "context", None)
    rows = P("dp", None)
    expert = P("expert", "dp", None)
    in_specs = (
        token,
        P(("expert", "dp"), "context"),
        token,
        token,
        token,
        token,
        P("dp"),
        rows,
        rows,
        rows,
        rows,
        P("dp"),
        rows,
        P(),
        rows,
        rows,
        expert,
        expert,
        expert,
    )
    out_specs = (
        token,
        token,
        P("dp"),
        rows,
        rows,
        rows,
        rows,
        P("dp"),
        rows,
        P(),
        rows,
        rows,
        expert,
        expert,
        expert,
    )
    return jax.shard_map(
        on_device, mesh=mesh, in_specs=in_specs, out_specs=out_specs, check_vma=False
    )
```

profile of v0, /device:TPU:19, one launch (start us, length us, event | category | flops | bytes accessed | tf_op | source)
XLA Modules:
  0.0 511.5 jit_solution(4476487330306872875)
XLA Ops:
  9.2 1.8 constant_dynamic-slice_fusion.1
  12.8 34.1 %spread.1 = (bf16[4,2,4,192,384]{4,3,2,1,0:T(8,128)(2,1)S(1)}, f32[4,16,192]{2,1,0:T(8,128)S(1)}) custom-call(bf16[192,768]{1,0:T(8,128)(2,1)S(1)} %copy-done.14, bf16[192,768]{1,0:T(8,128)(2,1)S(1)} %copy-done.15, bf16[192,768]{1,0:T(8,128)(2,1)S(1)} %copy-done.16, bf16[192,768]{1,0:T(8,128)(2,1)S(1)} %copy-done.17, ...), custom_call_target="tpu_custom_call" | custom-call | flops 1000000 | bytes 9437184 | tf_op jit(solution)/shard_map/spread/pallas_call | solution.py:193
  46.9 2.2 copy-done.5
  52.1 7.6 %project.1 = (bf16[2,3,1024,384]{3,2,1,0:T(8,128)(2,1)S(1)}, bf16[1024,768]{1,0:T(8,128)(2,1)S(1)}) custom-call(s32[1]{0:T(128)} %bitcast.8.ctx_ref, bf16[1024,768]{1,0:T(8,128)(2,1)S(1)} %bitcast.65, bf16[128,768]{1,0:T(8,128)(2,1)S(1)} %maximum_maximum_fusion.extra_ref, bf16[4,2,768,384]{3,2,1,0:T(8,128)(2,1)} %bitcast.58, f32[2048,128]{1,0:T(8,128)S(1)} %copy-done.26, ...), custom_call_target="tpu_custom_call" | custom-call | flops 3623878656 | bytes 12976128 | tf_op jit(solution)/shard_map/project/pallas_call | solution.py:277
  59.8 2.2 copy-done.4
  63.2 6.0 %all-to-all-start = ((bf16[2,3,1024,384]{3,2,1,0:T(8,128)(2,1)}), bf16[2,3,1024,384]{3,2,1,0:T(8,128)(2,1)}, u32[]{:S(2)}, u32[]{:S(2)}) async-start(bf16[2,3,1024,384]{3,2,1,0:T(8,128)(2,1)} %copy-done.4), calls=%async_computation | async-start | bytes 9437184 | tf_op jit(solution)/shard_map/all_to_all | solution.py:1396
  69.2 4.2 all-gather
  73.3 1.8 convert_reduce_fusion
  75.4 50.8 %attend.1 = (bf16[2,1024,384]{2,1,0:T(8,128)(2,1)S(1)}, f32[3,8,8,256]{3,2,1,0:T(8,128)S(1)}) custom-call(s32[8]{0:T(128)S(1)} %and_select_fusion.first_ref, bf16[2,3,1024,384]{3,2,1,0:T(8,128)(2,1)} %all-to-all-done.q_ref.k_ref.v_ref, bf16[2,3,1024,384]{3,2,1,0:T(8,128)(2,1)} %all-to-all-done.q_ref.k_ref.v_ref, ...), custom_call_target="tpu_custom_call" | custom-call | flops 40000000000 | bytes 6291456 | tf_op jit(solution)/shard_map/attend/pallas_call | solution.py:375
  127.4 4.1 all-to-all-start.1
  132.2 2.1 place.1
  135.2 2.9 copy-done.6
  140.5 5.4 %middle.1 = (f32[1024,768]{1,0:T(8,128)S(1)}, bf16[1024,768]{1,0:T(8,128)(2,1)S(1)}, f32[1024,128]{1,0:T(8,128)S(1)}) custom-call(bf16[1024,768]{1,0:T(8,128)(2,1)S(1)} %bitcast.66, bf16[2,1024,384]{2,1,0:T(8,128)(2,1)S(1)} %all-to-all-done.1.o_ref, bf16[4,2,768,384]{3,2,1,0:T(8,128)(2,1)S(1)} %bitcast.61, bf16[128,768]{1,0:T(8,128)(2,1)S(1)} %copy-done.13, ...), custom_call_target="tpu_custom_call" | custom-call | flops 1207959552 | bytes 9043968 | tf_op jit(solution)/shard_map/middle/pallas_call | solution.py:573
  145.9 1.7 copy-done.19
  149.5 88.1 %experts.1 = (bf16[4,288,768]{2,1,0:T(8,128)(2,1)}, bf16[4,288,768]{2,1,0:T(8,128)(2,1)}, bf16[4,768,256]{2,1,0:T(8,128)(2,1)}, bf16[4,768,256]{2,1,0:T(8,128)(2,1)}, bf16[8,256,384]{2,1,0:T(8,128)(2,1)}) custom-call(f32[8,1024]{1,0:T(8,128)} %copy-done.23, bf16[1024,768]{1,0:T(8,128)(2,1)} %copy-done.20, bf16[1024,768]{1,0:T(8,128)(2,1)} %bitcast.83, ...), custom_call_target="tpu_custom_call" | custom-call | flops 32614907904 | bytes 47185920 | tf_op jit(solution)/shard_map/experts/pallas_call | solution.py:869
  237.6 1.7 copy.63
  239.3 1.6 copy.67
  241.0 1.7 copy.64
  242.7 1.6 copy.69
  244.4 34.3 %combine.1 = (bf16[1024,768]{1,0:T(8,128)(2,1)}, f32[1024,768]{1,0:T(8,128)}, bf16[2,1024,384]{2,1,0:T(8,128)(2,1)}, bf16[2,768,384]{2,1,0:T(8,128)(2,1)}, f32[24,768]{1,0:T(8,128)}) custom-call(bf16[1152,768]{1,0:T(8,128)(2,1)} %bitcast.86, bf16[1152,768]{1,0:T(8,128)(2,1)} %bitcast.87, s32[1024,128]{1,0:T(8,128)} %copy-done.21, f32[1024,128]{1,0:T(8,128)} %copy-done.22, ...), custom_call_target="tpu_custom_call" | custom-call | flops 7851737088 | bytes 28311552 | tf_op jit(solution)/shard_map/combine/pallas_call | solution.py:1041
  278.7 5.8 %all-to-all-start.2 = ((bf16[2,1024,384]{2,1,0:T(8,128)(2,1)}), bf16[2,1024,384]{2,1,0:T(8,128)(2,1)}, u32[]{:S(2)}, u32[]{:S(2)}) async-start(bf16[2,1024,384]{2,1,0:T(8,128)(2,1)} %get-tuple-element.53), calls=%async_computation.2 | async-start | bytes 3145728 | tf_op jit(solution)/shard_map/all_to_all | solution.py:1396
  285.1 1.7 all-to-all-done.2.do_ref
  288.0 63.4 %attend_back.1 = bf16[2,3,1024,384]{3,2,1,0:T(8,128)(2,1)} custom-call(s32[8]{0:T(128)S(1)} %and_select_fusion.first_ref, bf16[2,3,1024,384]{3,2,1,0:T(8,128)(2,1)} %all-to-all-done.q_ref.k_ref.v_ref, bf16[2,3,1024,384]{3,2,1,0:T(8,128)(2,1)} %all-to-all-done.q_ref.k_ref.v_ref, bf16[2,3,1024,384]{3,2,1,0:T(8,128)(2,1)} %all-to-all-done.q_ref.k_ref.v_ref, ...), custom_call_target="tpu_custom_call" | custom-call | flops 99999997952 | bytes 12582912 | tf_op jit(solution)/shard_map/attend_back/pallas_call | solution.py:501
  351.5 12.7 %all_to_all.20.g_ref = bf16[2,3,1024,384]{3,2,1,0:T(8,128)(2,1)} all-to-all(bf16[2,3,1024,384]{3,2,1,0:T(8,128)(2,1)} %attend_back.1), channel_id=1, replica_groups=mesh['expert'=4,'context'=2,'dp'=4] {'context'}, dimensions={0} | all-to-all | bytes 9437184 | tf_op jit(solution)/shard_map/all_to_all | solution.py:1396
  364.2 21.0 %project_back.1 = (f32[1024,768]{1,0:T(8,128)}, bf16[2,4,768,384]{3,2,1,0:T(8,128)(2,1)}, f32[1,768]{1,0:T(1,128)}) custom-call(bf16[2,3,1024,384]{3,2,1,0:T(8,128)(2,1)} %all_to_all.20.g_ref, bf16[4,2,768,384]{3,2,1,0:T(8,128)(2,1)} %bitcast.60, bf16[128,768]{1,0:T(8,128)(2,1)} %copy-done.12, bf16[1024,768]{1,0:T(8,128)(2,1)} %bitcast.64, ...), custom_call_target="tpu_custom_call" | custom-call | flops 7247757312 | bytes 26345472 | tf_op jit(solution)/shard_map/project_back/pallas_call | solution.py:1131
  385.2 94.1 %reduce_shared.1 = (f32[4,192,768]{2,1,0:T(8,128)}, f32[24,768]{1,0:T(8,128)}) custom-call(bf16[2,4,4,192,384]{4,3,2,1,0:T(8,128)(2,1)} %bitcast.71, f32[24,768]{1,0:T(8,128)} %get-tuple-element.60.small_ref, f32[1,768]{1,0:T(1,128)} %get-tuple-element.61.gain_ref), custom_call_target="tpu_custom_call" | custom-call | flops 1000000 | bytes 4718592 | tf_op jit(solution)/shard_map/reduce_shared/pallas_call | solution.py:1358
  486.1 3.0 slice_bitcast_fusion
  490.4 2.6 all_gather.28
  493.1 1.7 copy.65
  496.0 2.6 all_gather.29
  498.7 1.7 copy.66
  500.4 2.6 all_gather.30
  (130 shorter events, 27.6 us)
Async XLA Ops:
  7.2 142.3 %all-gather.5.cloned.1.call-start = ((), (), s32[]{:S(2)}) async-start(), calls=%async_computation.7 | async-start | bytes 3538944 | tf_op jit(solution)/shard_map/all_gather | solution.py:1435
  8.3 3.7 copy-start.39
  8.3 4.4 copy-start.34
  8.3 4.4 copy-start.36
  8.3 4.4 copy-start.38
  8.3 4.4 copy-start.14
  8.3 4.4 copy-start.15
  8.4 4.4 copy-start.16
  8.4 4.4 copy-start.17
  9.2 140.3 %all-gather.7.cloned.1.call-start = ((), (), s32[]{:S(2)}) async-start(), calls=%async_computation.8 | async-start | bytes 3538944 | tf_op jit(solution)/shard_map/all_gather | solution.py:1435
  11.1 38.5 %copy-start.10 = (bf16[1,1024,768]{2,1,0:T(8,128)(2,1)S(1)}, bf16[1,1024,768]{2,1,0:T(8,128)(2,1)}, u32[]{:S(2)}) copy-start(bf16[1,1024,768]{2,1,0:T(8,128)(2,1)} %param.21) | copy-start | bytes 4718596
  11.1 138.4 %all-gather.9.cloned.1.call-start = ((), (), s32[]{:S(2)}) async-start(), calls=%async_computation.9 | async-start | bytes 3538944 | tf_op jit(solution)/shard_map/all_gather | solution.py:1435
  49.6 10.2 %copy-start.12 = (bf16[128,768]{1,0:T(8,128)(2,1)}, bf16[128,768]{1,0:T(8,128)(2,1)S(1)}, u32[]{:S(2)}) copy-start(bf16[128,768]{1,0:T(8,128)(2,1)S(1)} %maximum_maximum_fusion.extra_ref) | copy-start | bytes 589828
  63.2 6.0 %copy-start.35 = (s32[1,1024]{1,0:T(1,128)S(1)}, s32[1,1024]{1,0:T(1,128)}, u32[]{:S(2)}) copy-start(s32[1,1024]{1,0:T(1,128)} %param.22) | copy-start | bytes 12292
  63.2 12.3 %all-to-all-start = ((bf16[2,3,1024,384]{3,2,1,0:T(8,128)(2,1)}), bf16[2,3,1024,384]{3,2,1,0:T(8,128)(2,1)}, u32[]{:S(2)}, u32[]{:S(2)}) async-start(bf16[2,3,1024,384]{3,2,1,0:T(8,128)(2,1)} %copy-done.4), calls=%async_computation | async-start | bytes 9437184 | tf_op jit(solution)/shard_map/all_to_all | solution.py:1396
  127.4 4.2 copy-start.29
  127.4 4.2 copy-start.33
  127.4 4.4 copy-start.32
  127.4 4.6 copy-start.18
  127.4 7.8 %all-to-all-start.1 = ((bf16[2,1024,384]{2,1,0:T(8,128)(2,1)}), bf16[2,1024,384]{2,1,0:T(8,128)(2,1)S(1)}, u32[]{:S(2)}, u32[]{:S(2)}) async-start(bf16[2,1024,384]{2,1,0:T(8,128)(2,1)} %copy-done.8), calls=%async_computation.1 | async-start | bytes 3145728 | tf_op jit(solution)/shard_map/all_to_all | solution.py:1396
  131.5 357.6 %reduce-scatter.10.cloned.1.call-start = ((), (), s32[]{:S(2)}) async-start(), calls=%async_computation.11 | async-start | bytes 1966080
  131.8 14.1 %copy-start.3 = (s32[1,1024,2]{2,1,0:T(8,128)}, s32[1,1024,2]{2,1,0:T(8,128)S(1)}, u32[]{:S(2)}) copy-start(s32[1,1024,2]{2,1,0:T(8,128)S(1)} %copy.58) | copy-start | bytes 24580
  132.0 13.9 %copy-start.7 = (f32[1,1024,8]{2,1,0:T(8,128)}, f32[1,1024,8]{2,1,0:T(8,128)S(1)}, u32[]{:S(2)}) copy-start(f32[1,1024,8]{2,1,0:T(8,128)S(1)} %copy.62) | copy-start | bytes 98308
  135.2 10.7 %copy-start.23 = (f32[8,1024]{1,0:T(8,128)}, f32[8,1024]{1,0:T(8,128)S(1)}, u32[]{:S(2)}) copy-start(f32[8,1024]{1,0:T(8,128)S(1)} %get-tuple-element.41.flat_ref) | copy-start | bytes 98308
  135.2 10.7 %copy-start.2 = (bf16[2,1024,384]{2,1,0:T(8,128)(2,1)}, bf16[2,1024,384]{2,1,0:T(8,128)(2,1)S(1)}, u32[]{:S(2)}) copy-start(bf16[2,1024,384]{2,1,0:T(8,128)(2,1)S(1)} %all-to-all-done.1.o_ref) | copy-start | bytes 4718596
  241.0 253.8 %reduce-scatter.12.cloned.1.call-start = ((), (), s32[]{:S(2)}) async-start(), calls=%async_computation.12 | async-start | bytes 1966080
  278.7 8.1 %copy-start.9 = (bf16[2,1024,384]{2,1,0:T(8,128)(2,1)S(1)}, bf16[2,1024,384]{2,1,0:T(8,128)(2,1)}, u32[]{:S(2)}) copy-start(bf16[2,1024,384]{2,1,0:T(8,128)(2,1)} %copy-done.8) | copy-start | bytes 4718596
  278.7 8.1 %copy-start.24 = (f32[2,1024,128]{2,1,0:T(8,128)S(1)}, f32[2,1024,128]{2,1,0:T(8,128)}, u32[]{:S(2)}) copy-start(f32[2,1024,128]{2,1,0:T(8,128)} %constant.68.cos_ref) | copy-start | bytes 3145732
  278.7 8.1 %copy-start.30 = (f32[3,8,8,256]{3,2,1,0:T(8,128)S(1)}, f32[3,8,8,256]{3,2,1,0:T(8,128)}, u32[]{:S(2)}) copy-start(f32[3,8,8,256]{3,2,1,0:T(8,128)} %copy-done.29) | copy-start | bytes 589828
  278.7 8.1 %all-to-all-start.2 = ((bf16[2,1024,384]{2,1,0:T(8,128)(2,1)}), bf16[2,1024,384]{2,1,0:T(8,128)(2,1)}, u32[]{:S(2)}, u32[]{:S(2)}) async-start(bf16[2,1024,384]{2,1,0:T(8,128)(2,1)} %get-tuple-element.53), calls=%async_computation.2 | async-start | bytes 3145728 | tf_op jit(solution)/shard_map/all_to_all | solution.py:1396
  284.6 215.9 %reduce-scatter.8.cloned.1.call-start = ((), (), s32[]{:S(2)}) async-start(), calls=%async_computation.10 | async-start | bytes 1966080 | tf_op jit(solution)/shard_map/reduce_scatter | solution.py:1482
  498.7 5.5 %copy-start.1 = (bf16[1,192,2048]{2,1,0:T(8,128)(2,1)S(1)}, bf16[1,192,2048]{2,1,0:T(8,128)(2,1)}, u32[]{:S(2)}) copy-start(bf16[1,192,2048]{2,1,0:T(8,128)(2,1)} %param.37) | copy-start | bytes 2359300
  (17 other events, 26.9 us)
Sparse Core Ops, SparseCore 0:
  10.2 46.1 all-gather.4
  58.0 39.5 all-gather.6
  99.2 37.1 all-gather.8
  241.1 59.9 reduce-scatter.9
  303.2 34.2 reduce-scatter.11
  339.7 34.2 reduce-scatter.7
where the time goes:
time: 515 us; the launch traced here: 512 us
  Pallas kernels  401 us (78%)
  local copies, waits for them, and re-layouts  49 us (10%)
  blocking collectives  24.6 us (5%)
  starting transfers between devices  16.1 us (3%)
  between operations  15.1 us (3%)
    pallas_call x1, Pallas kernels, reduce_shared(): pl.pallas_call(functools.partial(reduce_kernel, gain_at), in_specs=[vmem]...  94.1 us
    pallas_call x1, Pallas kernels, run_experts(): pl.pallas_call(functools.partial(expert_kernel, total), in_specs=[vmem] *...  88.1 us
    pallas_call x1, Pallas kernels, attend_back(): pl.pallas_call(attend_back_kernel, grid_spec=pltpu.PrefetchScalarGridSpec...  63.4 us
    pallas_call x1, Pallas kernels, attend(): pl.pallas_call(attend_kernel, grid_spec=pltpu.PrefetchScalarGridSpec(num_...  50.8 us
    pallas_call x1, Pallas kernels, combine(): pl.pallas_call(functools.partial(combine_kernel, experts, total), grid=(r...  34.3 us
    pallas_call x1, Pallas kernels, spread(): pl.pallas_call(spread_kernel, in_specs=[vmem] * 5, out_specs=[vmem] * 2,...  34.1 us
    unnamed x88, local copies, waits for them, and re-layouts  30.7 us
    pallas_call x1, Pallas kernels, project_back(): pl.pallas_call(project_back_kernel, grid=(rows // TB,), in_specs=[pl.Bloc...  21 us
  transfers between devices with their start and end apart: 9, of which 1 were waited for; matrix products, arithmetic and copies ran while one was open for 5% of the time, Pallas kernels for 61%

commit v1 on v0

--- a/solution.py
+++ b/solution.py
@@ -12,6 +12,7 @@
 HEAD_DIM = 64
 WIN = 1024
 NZ = 4
+SEGMENTS = 5
 GAIN_ONE, GAIN_TWO, VECS = 112, 113, 114
 TQ = 256
 TB = 256
@@ -106,18 +107,71 @@
     pl.semaphore_wait(barrier, total)
 
 
+def place_pairs(experts, cap, routes_ref, ranks_ref, flat_ref, flat_t_ref):
+    rows = routes_ref.shape[0]
+    lane = iota((rows, LANES), 1)
+    first, second = routes_ref[:, 0:1], routes_ref[:, 1:2]
+    hot_first, hot_second = first == lane, second == lane
+    hot = (hot_first.astype(F32) + hot_second.astype(F32)).astype(BF16)
+    ranks = ranks_ref[...].astype(F32)
+    ranks_col = jnp.broadcast_to(ranks, (LANES, rows)).T[:, 0:1]
+    earlier = jnp.where(ranks < ranks_col, 1.0, 0.0).astype(BF16)
+    counts = dot(earlier, hot)
+
+    def flat(hit, route):
+        slot = jnp.sum(jnp.where(hit, counts, 0.0), axis=1, keepdims=True).astype(jnp.int32)
+        return jnp.where((route < experts) & (slot < cap), route * cap + slot, experts * cap)
+
+    out = jnp.where(
+        lane == 0, flat(hot_first, first), jnp.where(lane == 1, flat(hot_second, second), 0)
+    )
+    flat_ref[...] = out
+    flat_t_ref[...] = out.astype(F32).T[:8]
+
+
+def find_starts(segs_ref, low_ref, first_ref):
+    rows = segs_ref.shape[2]
+    per = rows // TQ
+    segs = [segs_ref[side].astype(F32) for side in range(2)]
+    starts = [jnp.zeros((1, rows), F32) for side in range(2)]
+    for number in range(1, SEGMENTS):
+        before = sum(
+            jnp.sum(jnp.where(part < number, 1.0, 0.0), axis=1, keepdims=True) for part in segs
+        )
+        starts = [
+            jnp.where(part == number, before, start) for part, start in zip(segs, starts)
+        ]
+    for side in range(2):
+        place = (iota((1, rows), 1) + (side * rows - WIN + 1)).astype(F32)
+        low = jnp.maximum(starts[side], place)
+        for tile in range(per):
+            part = low[:, tile * TQ : (tile + 1) * TQ]
+            low_ref[side * per + tile] = part.astype(jnp.int32)
+            first_ref[side * per + tile] = jnp.min(part).astype(jnp.int32) // TQ
+
+
 def spread_kernel(
+    cap,
     w_query_ref,
     w_key_ref,
     w_value_ref,
     w_out_ref,
     extra_ref,
+    routes_ref,
+    ranks_ref,
+    segs_ref,
     out_ref,
     extra_out_ref,
+    flat_ref,
+    flat_t_ref,
+    low_ref,
+    first_ref,
+    segs_all,
     slab_sems,
     plane_sems,
     core_sems,
     extra_sems,
+    segs_sems,
 ):
     experts = lax.axis_size("expert")
     slabs = lax.axis_size("dp")
@@ -131,6 +185,7 @@
                 out_ref[which, side, slab] = ref[:, side * half : (side + 1) * half]
 
     extra_out_ref[slab] = extra_ref[...]
+    segs_all[core] = segs_ref[...]
     greet_all(("context", "expert", "dp"))
 
     def slab_copy(k):
@@ -159,6 +214,13 @@
     loop(slabs - 1, lambda k: extra_copy(k).start())
     loop(slabs - 1, lambda k: slab_copy(k).start())
     share(slab)
+    segs_copy = remote(
+        segs_all.at[core], segs_all.at[core], segs_sems, (0,), {"context": 1 - core}
+    )
+    segs_copy.start()
+    place_pairs(experts, cap, routes_ref, ranks_ref, flat_ref, flat_t_ref)
+    segs_copy.wait()
+    find_starts(segs_all, low_ref, first_ref)
 
     def forward(k):
         slab_copy(k).wait_recv()
@@ -185,65 +247,39 @@
     loop(slabs, finish)
 
 
-def spread(experts, slabs, w_query, w_key, w_value, w_out, extra):
+def spread(experts, slabs, cap, w_query, w_key, w_value, w_out, extra, routes, ranks, segs):
+    tokens = routes.shape[0]
+    tiles = 2 * tokens // TQ
     rows, width = w_query.shape
     half = width // 2
     vmem = pl.BlockSpec(memory_space=pltpu.VMEM)
     dma = pltpu.SemaphoreType.DMA
     return pl.pallas_call(
-        spread_kernel,
-        in_specs=[vmem] * 5,
-        out_specs=[vmem] * 2,
+        functools.partial(spread_kernel, cap),
+        in_specs=[vmem] * 8,
+        out_specs=[vmem] * 5 + [pl.BlockSpec(memory_space=pltpu.SMEM)],
         out_shape=(
             jax.ShapeDtypeStruct((4, 2, slabs, rows, half), BF16),
             jax.ShapeDtypeStruct((slabs,) + extra.shape, F32),
+            jax.ShapeDtypeStruct((tokens, LANES), jnp.int32),
+            jax.ShapeDtypeStruct((8, tokens), F32),
+            jax.ShapeDtypeStruct((tiles, 1, TQ), jnp.int32),
+            jax.ShapeDtypeStruct((tiles,), jnp.int32),
         ),
         scratch_shapes=[
+            pltpu.VMEM((2, 1, tokens), jnp.int32),
             dma((2, slabs - 1)),
             dma((2, experts - 1, slabs)),
             dma((2, experts, slabs)),
             dma((2, slabs - 1)),
+            dma((2, 1)),
         ],
         compiler_params=pltpu.CompilerParams(
             collective_id=1, has_side_effects=True, vmem_limit_bytes=32 * MIB
         ),
         cost_estimate=cost(1e6, 16 * width * width),
         name="spread",
-    )(w_query, w_key, w_value, w_out, extra)
-
-
-def place_kernel(experts, cap, routes_ref, rank_col_ref, rank_row_ref, flat_ref, flat_t_ref):
-    rows = routes_ref.shape[0]
-    lane = iota((rows, LANES), 1)
-    first, second = routes_ref[:, 0:1], routes_ref[:, 1:2]
-    hot_first, hot_second = first == lane, second == lane
-    hot = (hot_first.astype(F32) + hot_second.astype(F32)).astype(BF16)
-    earlier = jnp.where(rank_row_ref[...] < rank_col_ref[...], 1.0, 0.0).astype(BF16)
-    counts = dot(earlier, hot)
-
-    def flat(hit, route):
-        slot = jnp.sum(jnp.where(hit, counts, 0.0), axis=1, keepdims=True).astype(jnp.int32)
-        return jnp.where((route < experts) & (slot < cap), route * cap + slot, experts * cap)
-
-    out = jnp.where(
-        lane == 0, flat(hot_first, first), jnp.where(lane == 1, flat(hot_second, second), 0)
-    )
-    flat_ref[...] = out
-    flat_t_ref[...] = out.astype(F32).T[:8]
-
-
-def place(routes, ranks, experts, cap):
-    rows = routes.shape[0]
-    return pl.pallas_call(
-        functools.partial(place_kernel, experts, cap),
-        out_shape=(
-            jax.ShapeDtypeStruct((rows, LANES), jnp.int32),
-            jax.ShapeDtypeStruct((8, rows), F32),
-        ),
-        compiler_params=params(32),
-        cost_estimate=cost(2 * rows * rows * LANES, 8 * rows * LANES),
-        name="place",
-    )(routes, ranks.reshape(rows, 1), ranks.reshape(1, rows))
+    )(w_query, w_key, w_value, w_out, extra, routes, ranks, segs)
 
 
 def qkv_kernel(ctx_ref, x_ref, extra_ref, w_ref, cos_ref, sin_ref, out_ref, aone_ref, whole_ref):
@@ -308,60 +344,68 @@
     return low, (1.0 - low.astype(F32)).astype(BF16)
 
 
-def attend_kernel(first_ref, q_ref, k_ref, v_ref, lo_ref, o_ref, lse_ref, vt_ref):
-    per = q_ref.shape[2] // TQ
-    count = 2 * per
+def spans(tile, first, body):
+    for count in range(1, WIN // TQ + 2):
+
+        @pl.when(tile - first + 1 == count)
+        def _():
+            body(count)
+
+
+def allowed(low, start, count):
+    sub = iota((TQ, TQ), 0)
+    marks = [sub >= low - (start + t * TQ) for t in range(count)]
+    marks[-1] = marks[-1] & (sub <= iota((TQ, TQ), 1))
+    return marks
+
+
+def masked(scores, marks):
+    return [
+        jnp.where(mark, scores[t * TQ : (t + 1) * TQ], MASKED) for t, mark in enumerate(marks)
+    ]
+
+
+def attend_kernel(first_ref, q_ref, k_ref, v_ref, lo_ref, o_ref, lse_ref, keys_ref, vt_ref):
+    rows = q_ref.shape[2]
+    per = rows // TQ
     masks = head_masks()
-    sub = iota((TQ, TQ), 0)
-    diagonal = sub <= iota((TQ, TQ), 1)
-
-    def turn(tile, carry):
-        vt_ref[tile] = v_ref[tile // per, 0, pl.ds((tile % per) * TQ, TQ), :].T
+    for side in range(2):
+        at = slice(side * rows, (side + 1) * rows)
+        keys_ref[at, :] = k_ref[side, 0]
+        turned = v_ref[side, 0].T
+        for head in range(2):
+            vt_ref[head, :HEAD_DIM, at] = turned[head * HEAD_DIM : (head + 1) * HEAD_DIM]
+            vt_ref[head, HEAD_DIM:, at] = jnp.ones((16, rows), BF16)
+
+    def q_step(qi, carry):
+        at = pl.ds(pl.multiple_of(lax.rem(qi, per) * TQ, TQ), TQ)
+        query = q_ref[qi // per, 0, at, :]
+        low = lo_ref[qi]
+
+        def run(count):
+            start = pl.multiple_of((qi - count + 1) * TQ, TQ)
+            span = pl.ds(start, count * TQ)
+            keys = keys_ref[span, :]
+            marks = allowed(low, start, count)
+            outs = []
+            for head in range(2):
+                scores = masked(dot_nt(keys, query * masks[head]), marks)
+                peak = functools.reduce(
+                    jnp.maximum, [jnp.max(part, axis=0, keepdims=True) for part in scores]
+                )
+                probs = jnp.concatenate(
+                    [jnp.exp(part - peak).astype(BF16) for part in scores], axis=0
+                )
+                mixed = dot(vt_ref[head, :, span], probs)
+                total = mixed[HEAD_DIM : HEAD_DIM + 1]
+                outs.append(mixed[:HEAD_DIM] / total)
+                lse_ref[0, qi, head : head + 1, :] = peak + jnp.log(total)
+            o_ref[qi // per, at, :] = jnp.concatenate(outs, axis=0).T.astype(BF16)
+
+        spans(qi, first_ref[qi], run)
         return carry
 
-    lax.fori_loop(0, count, turn, 0)
-
-    def q_step(qi, carry):
-        rows = pl.ds((qi % per) * TQ, TQ)
-        query = q_ref[qi // per, 0, rows, :]
-        queries = [query * mask for mask in masks]
-        low = lo_ref[qi]
-        keys = k_ref[qi // per, 0, rows, :]
-        turned = vt_ref[qi]
-        ok = diagonal & (sub >= low - qi * TQ)
-        state = []
-        for head in range(2):
-            scores = jnp.where(ok, dot_nt(keys, queries[head]), MASKED)
-            peak = jnp.max(scores, axis=0, keepdims=True)
-            probs = jnp.exp(scores - peak)
-            total = jnp.sum(probs, axis=0, keepdims=True)
-            mixed = dot(turned[head * HEAD_DIM : (head + 1) * HEAD_DIM], probs.astype(BF16))
-            state += [peak, total, mixed]
-
-        def k_step(ki, state):
-            keys = k_ref[ki // per, 0, pl.ds((ki % per) * TQ, TQ), :]
-            turned = vt_ref[ki]
-            ok = sub >= low - ki * TQ
-            new = []
-            for head in range(2):
-                peak, total, mixed = state[3 * head : 3 * head + 3]
-                scores = jnp.where(ok, dot_nt(keys, queries[head]), MASKED)
-                top = jnp.maximum(peak, jnp.max(scores, axis=0, keepdims=True))
-                shrink = jnp.exp(peak - top)
-                probs = jnp.exp(scores - top)
-                total = total * shrink + jnp.sum(probs, axis=0, keepdims=True)
-                part = dot(turned[head * HEAD_DIM : (head + 1) * HEAD_DIM], probs.astype(BF16))
-                new += [top, total, mixed * shrink + part]
-            return tuple(new)
-
-        state = lax.fori_loop(first_ref[qi], qi, k_step, tuple(state))
-        out = jnp.concatenate([state[2] / state[1], state[5] / state[4]], axis=0)
-        o_ref[qi // per, rows, :] = out.T.astype(BF16)
-        lse_ref[0, qi, 0:1, :] = state[0] + jnp.log(state[1])
-        lse_ref[0, qi, 1:2, :] = state[3] + jnp.log(state[4])
-        return carry
-
-    lax.fori_loop(0, count, q_step, 0)
+    lax.fori_loop(0, 2 * per, q_step, 0)
 
 
 def part_spec(which, rows):
@@ -387,7 +431,10 @@
                 pl.BlockSpec((2, rows, LANES), lambda p, first: (0, 0, p)),
                 pl.BlockSpec((1, tiles, 8, TQ), lambda p, first: (p, 0, 0, 0)),
             ],
-            scratch_shapes=[pltpu.VMEM((tiles, LANES, TQ), BF16)],
+            scratch_shapes=[
+                pltpu.VMEM((2 * rows, LANES), BF16),
+                pltpu.VMEM((2, HEAD_DIM + 16, 2 * rows), BF16),
+            ],
         ),
         out_shape=(
             jax.ShapeDtypeStruct((2, rows, half), BF16),
@@ -411,85 +458,88 @@
     cos_ref,
     sin_ref,
     g_ref,
+    keys_ref,
+    values_ref,
     kt_ref,
     delta_ref,
     dk_ref,
     dv_ref,
 ):
-    per = q_ref.shape[2] // TQ
-    count = 2 * per
+    rows = q_ref.shape[2]
+    per = rows // TQ
     masks = head_masks()
-    sub = iota((TQ, TQ), 0)
-    diagonal = sub <= iota((TQ, TQ), 1)
+    for side in range(2):
+        at = slice(side * rows, (side + 1) * rows)
+        keys_ref[at, :] = k_ref[side, 0]
+        values_ref[at, :] = v_ref[side, 0]
+        kt_ref[:, at] = k_ref[side, 0].T
+    dk_ref[...] = jnp.zeros_like(dk_ref)
+    dv_ref[...] = jnp.zeros_like(dv_ref)
 
     def prepare(tile, carry):
-        rows = pl.ds((tile % per) * TQ, TQ)
-        kt_ref[tile] = k_ref[tile // per, 0, rows, :].T
-        both = o_ref[tile // per, rows, :].astype(F32) * do_ref[tile // per, rows, :].astype(F32)
+        at = pl.ds(pl.multiple_of(lax.rem(tile, per) * TQ, TQ), TQ)
+        both = o_ref[tile // per, at, :].astype(F32) * do_ref[tile // per, at, :].astype(F32)
         both = both.T
         delta_ref[tile, 0:1, :] = jnp.sum(both[:HEAD_DIM], axis=0, keepdims=True)
         delta_ref[tile, 1:2, :] = jnp.sum(both[HEAD_DIM:], axis=0, keepdims=True)
-        dk_ref[tile] = jnp.zeros((TQ, LANES), F32)
-        dv_ref[tile] = jnp.zeros((TQ, LANES), F32)
         return carry
 
-    lax.fori_loop(0, count, prepare, 0)
+    lax.fori_loop(0, 2 * per, prepare, 0)
 
     def q_step(qi, carry):
-        rows = pl.ds((qi % per) * TQ, TQ)
-        query = q_ref[qi // per, 0, rows, :]
-        grad = do_ref[qi // per, rows, :]
-        queries = [query * mask for mask in masks]
-        grads = [grad * mask for mask in masks]
-        both_queries = jnp.concatenate(queries, axis=0)
-        both_grads = jnp.concatenate(grads, axis=0)
+        at = pl.ds(pl.multiple_of(lax.rem(qi, per) * TQ, TQ), TQ)
+        query = q_ref[qi // per, 0, at, :]
+        grad = do_ref[qi // per, at, :]
         low = lo_ref[qi]
-        lse = [lse_ref[0, qi, h : h + 1, :] for h in range(2)]
-        delta = [delta_ref[qi, h : h + 1, :] for h in range(2)]
-
-        def tile(ki, ok, sums):
-            at = pl.ds((ki % per) * TQ, TQ)
-            keys = k_ref[ki // per, 0, at, :]
-            values = v_ref[ki // per, 0, at, :]
-            turned = kt_ref[ki]
-            all_probs, all_scores, new = [], [], []
+
+        def run(count):
+            start = pl.multiple_of((qi - count + 1) * TQ, TQ)
+            span = pl.ds(start, count * TQ)
+            keys, values = keys_ref[span, :], values_ref[span, :]
+            marks = allowed(low, start, count)
+            queries = [query * mask for mask in masks]
+            grads = [grad * mask for mask in masks]
+            all_probs, all_scores, sums = [], [], []
             for h in range(2):
-                scores = jnp.where(ok, dot_nt(keys, queries[h]), MASKED)
-                probs = jnp.exp(scores - lse[h])
+                lse = lse_ref[0, qi, h : h + 1, :]
+                delta = delta_ref[qi, h : h + 1, :]
+                scores = masked(dot_nt(keys, queries[h]), marks)
                 grad_probs = dot_nt(values, grads[h])
-                grad_scores = (probs * (grad_probs - delta[h])).astype(BF16)
-                new.append(
-                    sums[h] + dot(turned[h * HEAD_DIM : (h + 1) * HEAD_DIM], grad_scores)
-                )
-                all_probs.append(probs.astype(BF16))
-                all_scores.append(grad_scores)
-            dv_ref[ki] += dot(jnp.concatenate(all_probs, axis=1), both_grads)
-            dk_ref[ki] += dot(jnp.concatenate(all_scores, axis=1), both_queries)
-            return tuple(new)
-
-        start = jnp.zeros((HEAD_DIM, TQ), F32)
-        sums = tile(qi, diagonal & (sub >= low - qi * TQ), (start, start))
-        sums = lax.fori_loop(
-            first_ref[qi], qi, lambda ki, s: tile(ki, sub >= low - ki * TQ, s), sums
-        )
-        grad_query = jnp.concatenate(sums, axis=0).T * HEAD_DIM ** (-0.5)
-        cos, sin = cos_ref[qi // per, rows, :], sin_ref[qi // per, rows, :]
-        g_ref[qi // per, 0, rows, :] = (grad_query * cos - swap_halves(grad_query) * sin).astype(
-            BF16
-        )
+                probs = [jnp.exp(part - lse) for part in scores]
+                grad_scores = [
+                    (part * (grad_probs[t * TQ : (t + 1) * TQ] - delta)).astype(BF16)
+                    for t, part in enumerate(probs)
+                ]
+                all_probs.append(jnp.concatenate([part.astype(BF16) for part in probs], axis=0))
+                all_scores.append(jnp.concatenate(grad_scores, axis=0))
+                sums.append(dot(kt_ref[h * HEAD_DIM : (h + 1) * HEAD_DIM, span], all_scores[h]))
+            dv_ref[span, :] += dot(
+                jnp.concatenate(all_probs, axis=1), jnp.concatenate(grads, axis=0)
+            )
+            dk_ref[span, :] += dot(
+                jnp.concatenate(all_scores, axis=1), jnp.concatenate(queries, axis=0)
+            )
+            grad_query = jnp.concatenate(sums, axis=0).T * HEAD_DIM ** (-0.5)
+            cos, sin = cos_ref[qi // per, at, :], sin_ref[qi // per, at, :]
+            g_ref[qi // per, 0, at, :] = (
+                grad_query * cos - swap_halves(grad_query) * sin
+            ).astype(BF16)
+
+        spans(qi, first_ref[qi], run)
         return carry
 
-    lax.fori_loop(0, count, q_step, 0)
+    lax.fori_loop(0, 2 * per, q_step, 0)
 
     def finish(tile, carry):
-        rows = pl.ds((tile % per) * TQ, TQ)
-        cos, sin = cos_ref[tile // per, rows, :], sin_ref[tile // per, rows, :]
-        grad_key = dk_ref[tile]
-        g_ref[tile // per, 1, rows, :] = (grad_key * cos - swap_halves(grad_key) * sin).astype(BF16)
-        g_ref[tile // per, 2, rows, :] = dv_ref[tile].astype(BF16)
+        at = pl.ds(pl.multiple_of(lax.rem(tile, per) * TQ, TQ), TQ)
+        span = pl.ds(pl.multiple_of(tile * TQ, TQ), TQ)
+        cos, sin = cos_ref[tile // per, at, :], sin_ref[tile // per, at, :]
+        grad_key = dk_ref[span, :]
+        g_ref[tile // per, 1, at, :] = (grad_key * cos - swap_halves(grad_key) * sin).astype(BF16)
+        g_ref[tile // per, 2, at, :] = dv_ref[span, :].astype(BF16)
         return carry
 
-    lax.fori_loop(0, count, finish, 0)
+    lax.fori_loop(0, 2 * per, finish, 0)
 
 
 def attend_back(first, qkv, grad_o, o, lse, low, cos, sin):
@@ -516,10 +566,12 @@
             ],
             out_specs=pl.BlockSpec((2, 3, rows, LANES), lambda p, first: (0, 0, 0, p)),
             scratch_shapes=[
-                pltpu.VMEM((tiles, LANES, TQ), BF16),
+                pltpu.VMEM((2 * rows, LANES), BF16),
+                pltpu.VMEM((2 * rows, LANES), BF16),
+                pltpu.VMEM((LANES, 2 * rows), BF16),
                 pltpu.VMEM((tiles, 8, TQ), F32),
-                pltpu.VMEM((tiles, TQ, LANES), F32),
-                pltpu.VMEM((tiles, TQ, LANES), F32),
+                pltpu.VMEM((2 * rows, LANES), F32),
+                pltpu.VMEM((2 * rows, LANES), F32),
             ],
         ),
         out_shape=jax.ShapeDtypeStruct((2, 3, rows, half), BF16),
@@ -609,8 +661,7 @@
     wd_ref,
     flow_ref,
     drow_ref,
-    gg_ref,
-    gu_ref,
+    gw_ref,
     gd_ref,
     send_x,
     send_g,
@@ -821,8 +872,9 @@
     def keep(step, carry):
         gate, lift = products(step)
         wide_copy(step - per).wait_recv()
-        gg_ref[step - per] = (gate + wide_taken[step - per, 0].astype(F32)).astype(BF16)
-        gu_ref[step - per] = (lift + wide_taken[step - per, 1].astype(F32)).astype(BF16)
+        for i, value in enumerate((gate, lift)):
+            at = pl.ds(pl.multiple_of((i * per + step - per) * FC, FC), FC)
+            gw_ref[:, at] = (value + wide_taken[step - per, i].astype(F32)).astype(BF16)
         return carry
 
     lax.fori_loop(per, chunks, keep, 0)
@@ -869,12 +921,11 @@
     return pl.pallas_call(
         functools.partial(expert_kernel, total),
         in_specs=[vmem] * 4 + [anywhere] * 3,
-        out_specs=[anywhere] * 2 + [vmem] * 3,
+        out_specs=[anywhere] * 2 + [vmem] * 2,
         out_shape=(
             jax.ShapeDtypeStruct((experts, cap, width), BF16),
             jax.ShapeDtypeStruct((experts, cap, width), BF16),
-            jax.ShapeDtypeStruct((per, width, FC), BF16),
-            jax.ShapeDtypeStruct((per, width, FC), BF16),
+            jax.ShapeDtypeStruct((width, hidden), BF16),
             jax.ShapeDtypeStruct((chunks, FC, half), BF16),
         ),
         scratch_shapes=[
@@ -1078,103 +1129,43 @@
     )(flow, drow, flat, stat, routes, hres, atwo, dy, o, extra, w_shared, prev)
 
 
-def project_back_kernel(
-    g_ref, w_ref, extra_ref, x_ref, aone_ref, dh_ref, gwo_ref, out_ref, gw_ref, gain_out_ref, acc_ref
-):
-    step = pl.program_id(0)
-    half = g_ref.shape[3]
-    turned = aone_ref[...].T
-    dnone = None
-    for which in range(3):
-        grad = jnp.concatenate([g_ref[0, which], g_ref[1, which]], axis=1)
-        part = dot_nt(grad, jnp.concatenate([w_ref[which, 0], w_ref[which, 1]], axis=1))
-        dnone = part if dnone is None else dnone + part
-        weight = dot(turned, grad)
-
-        @pl.when(step == 0)
-        def _():
-            acc_ref[which] = weight
-
-        @pl.when(step > 0)
-        def _():
-            acc_ref[which] += weight
-
-    values = x_ref[...].astype(F32)
-    scale = lax.rsqrt(jnp.mean(values * values, axis=-1, keepdims=True) + EPS)
-    scaled = dnone * extra_ref[GAIN_ONE : GAIN_ONE + 1].astype(F32)
-    inner = jnp.mean(values * scaled, axis=1, keepdims=True)
-    out_ref[...] = dh_ref[...] + scale * scaled - values * (scale * scale * scale * inner)
-    row = jnp.sum(dnone * values * scale, axis=0, keepdims=True)
-
-    @pl.when(step == 0)
-    def _():
-        gain_out_ref[...] = row
-
-    @pl.when(step > 0)
-    def _():
-        gain_out_ref[...] += row
-
-    @pl.when(step == pl.num_programs(0) - 1)
-    def _():
-        for side in range(2):
-            for which in range(3):
-                at = side * half
-                gw_ref[side, which] = acc_ref[which, :, at : at + half].astype(BF16)
-            gw_ref[side, 3] = gwo_ref[side]
-
-
-def project_back(grad, w_shared, extra, x, aone, dh, grad_out_w):
-    rows, width = x.shape
-    half = width // 2
-    token = lambda i: (i, 0)
-    whole = lambda i: (0, 0)
-    return pl.pallas_call(
-        project_back_kernel,
-        grid=(rows // TB,),
-        in_specs=[
-            pl.BlockSpec((2, 3, TB, half), lambda i: (0, 0, i, 0)),
-            pl.BlockSpec((3, 2, width, half), lambda i: (0, 0, 0, 0)),
-            pl.BlockSpec((LANES, width), whole),
-            pl.BlockSpec((TB, width), token),
-            pl.BlockSpec((TB, width), token),
-            pl.BlockSpec((TB, width), token),
-            pl.BlockSpec((2, width, half), lambda i: (0, 0, 0)),
-        ],
-        out_specs=[
-            pl.BlockSpec((TB, width), token),
-            pl.BlockSpec((2, 4, width, half), lambda i: (0, 0, 0, 0)),
-            pl.BlockSpec((1, width), whole),
-        ],
-        out_shape=(
-            jax.ShapeDtypeStruct((rows, width), F32),
-            jax.ShapeDtypeStruct((2, 4, width, half), BF16),
-            jax.ShapeDtypeStruct((1, width), F32),
-        ),
-        scratch_shapes=[pltpu.VMEM((3, width, width), F32)],
-        compiler_params=params(56),
-        cost_estimate=cost(12 * rows * width * width, 18 * width * width + 20 * rows * width),
-        name="project_back",
-    )(grad, w_shared, extra, x, aone, dh, grad_out_w)
-
-
-def reduce_kernel(
+def tail_kernel(
     gain_at,
-    grads_ref,
+    sent_ref,
+    aone_ref,
+    w_ref,
+    extra_ref,
+    x_ref,
+    dh_ref,
+    gwo_ref,
     small_ref,
-    gain_ref,
+    wide_ref,
+    down_ref,
     out_ref,
+    final,
     small_out_ref,
+    wide_out,
+    down_out,
+    both,
+    grads,
+    w_buf,
+    x_buf,
+    dh_buf,
+    out_buf,
     core_in,
     plane_out,
     plane_in,
     slab_out,
     slab_in,
-    final,
     own_ref,
     small_own,
     small_core,
     small_plane,
     small_slab,
+    load_sems,
+    store_sems,
+    both_sems,
+    share_sems,
     core_sems,
     plane_sems,
     slab_sems,
@@ -1188,28 +1179,53 @@
     slabs = lax.axis_size("dp")
     me, core, slab = lax.axis_index("expert"), lax.axis_index("context"), lax.axis_index("dp")
     other = 1 - core
-
+    tokens, width = x_buf.shape
+    half = width // 2
+    parts = 2
+    block = tokens // parts
+
+    mine = pltpu.make_async_copy(sent_ref.at[core], both.at[core], load_sems.at[0])
+    mine.start()
+    loads = [
+        pltpu.make_async_copy(w_ref.at[pl.ds(0, 3)], w_buf, load_sems.at[1]),
+        pltpu.make_async_copy(x_ref, x_buf, load_sems.at[2]),
+        pltpu.make_async_copy(dh_ref, dh_buf, load_sems.at[3]),
+    ]
+    for copy in loads:
+        copy.start()
     greet_all(("context", "expert", "dp"))
-    send = remote
-
-    order = list(range(1, experts)) + [0]
-    core_copies = {}
-    for j in order:
-        core_copies[j] = send(
-            grads_ref.at[other, lax.rem(me + j, experts)],
-            core_in.at[j],
-            core_sems,
-            (j,),
+    theirs = [
+        remote(
+            sent_ref.at[other, which],
+            both.at[core, which],
+            both_sems,
+            (which,),
             {"context": other},
         )
-        core_copies[j].start()
-    row = iota(small_ref.shape, 0)
-    small_own[...] = small_ref[...] + jnp.where(row == gain_at, gain_ref[...], 0.0)
-    small_copy = send(small_own, small_core, small_core_sems, (0,), {"context": other})
-    small_copy.start()
+        for which in range(3)
+    ]
+    for copy in theirs:
+        copy.start()
+
+    def core_copy(which):
+        return remote(
+            grads.at[other, which], core_in.at[which], core_sems, (which,), {"context": other}
+        )
+
+    for side in range(2):
+        grads[side, 3] = gwo_ref[side]
+    core_copy(3).start()
+    wide_out[core] = wide_ref[...]
+    down_out[core] = down_ref[...]
+    shares = [
+        remote(ref.at[core], ref.at[core], share_sems, (i,), {"context": other})
+        for i, ref in enumerate((wide_out, down_out))
+    ]
+    for copy in shares:
+        copy.start()
 
     def plane_copy(j, at):
-        return send(
+        return remote(
             plane_out.at[j - 1, at],
             plane_in.at[j - 1, at],
             plane_sems,
@@ -1217,26 +1233,72 @@
             {"expert": lax.rem(me + j, experts)},
         )
 
-    for j in range(1, experts):
-        core_copies[j].wait_recv()
-        which = lax.rem(me + j, experts)
-
-        def pass_on(k, j=j, which=which):
-            at = lax.rem(slab + k + 1, slabs)
-            plane_out[j - 1, at] = (
-                grads_ref[core, which, at].astype(F32) + core_in[j, at].astype(F32)
-            ).astype(BF16)
-            plane_copy(j, at).start()
-
-        loop(slabs, pass_on)
-    core_copies[0].wait_recv()
-
+    def pass_on(which):
+        core_copy(which).wait_recv()
+        j = lax.rem(which + experts - me, experts)
+
+        @pl.when(j != 0)
+        def _():
+            def one(k):
+                at = lax.rem(slab + k + 1, slabs)
+                plane_out[j - 1, at] = (
+                    grads[core, which, at].astype(F32) + core_in[which, at].astype(F32)
+                ).astype(BF16)
+                plane_copy(j, at).start()
+
+            loop(slabs, one)
+
+    mine.wait()
+    turned = aone_ref[...].T
+    for which in range(3):
+        theirs[which].wait_recv()
+        grad = jnp.concatenate([both[0, which], both[1, which]], axis=1)
+        weight = dot(turned, grad)
+        for side in range(2):
+            grads[side, which] = (
+                weight[:, side * half : (side + 1) * half]
+                .reshape(slabs, width // slabs, half)
+                .astype(BF16)
+            )
+        core_copy(which).start()
+        pass_on((which + 3) % 4)
+    for copy in loads:
+        copy.wait()
+
+    gain = extra_ref[GAIN_ONE : GAIN_ONE + 1].astype(F32)
+    stores = []
+    gain_row = jnp.zeros((1, width), F32)
+    for part in range(parts):
+        at = slice(part * block, (part + 1) * block)
+        dnone = None
+        for which in range(3):
+            grad = jnp.concatenate([both[0, which, at], both[1, which, at]], axis=1)
+            whole = jnp.concatenate([w_buf[which, 0], w_buf[which, 1]], axis=1)
+            product = dot_nt(grad, whole)
+            dnone = product if dnone is None else dnone + product
+        values = x_buf[at].astype(F32)
+        scale = lax.rsqrt(jnp.mean(values * values, axis=-1, keepdims=True) + EPS)
+        scaled = dnone * gain
+        inner = jnp.mean(values * scaled, axis=1, keepdims=True)
+        out_buf[at] = dh_buf[at] + scale * scaled - values * (scale * scale * scale * inner)
+        stores.append(
+            pltpu.make_async_copy(out_buf.at[at], out_ref.at[at], store_sems.at[part])
+        )
+        stores[-1].start()
+        gain_row = gain_row + jnp.sum(dnone * values * scale, axis=0, keepdims=True)
+        if part == 0:
+            pass_on(2)
+
+    row = iota(small_ref.shape, 0)
+    small_own[...] = small_ref[...] + jnp.where(row == gain_at, gain_row, 0.0)
+    small_copy = remote(small_own, small_core, small_core_sems, (0,), {"context": other})
+    small_copy.start()
     small_copy.wait()
     small_plane[me] = small_own[...] + small_core[...]
     small_plane_copies = []
     for j in range(1, experts):
         small_plane_copies.append(
-            send(
+            remote(
                 small_plane.at[me],
                 small_plane.at[me],
                 small_plane_sems,
@@ -1247,14 +1309,14 @@
         small_plane_copies[-1].start()
 
     def gathered(at):
-        value = grads_ref[core, me, at].astype(F32) + core_in[0, at].astype(F32)
+        value = grads[core, me, at].astype(F32) + core_in[me, at].astype(F32)
         for j in range(1, experts):
             plane_copy(j, at).wait_recv()
             value = value + plane_in[j - 1, at].astype(F32)
         return value
 
     def slab_copy(k):
-        return send(
+        return remote(
             slab_out.at[k],
             slab_in.at[k],
             slab_sems,
@@ -1276,7 +1338,7 @@
     small_slab[slab] = value
 
     def small_slab_copy(k):
-        return send(
+        return remote(
             small_slab.at[slab],
             small_slab.at[slab],
             small_slab_sems,
@@ -1297,7 +1359,7 @@
     final_copies, pass_copies = [], []
     for j in range(1, experts):
         final_copies.append(
-            send(
+            remote(
                 final.at[core, me],
                 final.at[core, me],
                 final_sems,
@@ -1311,7 +1373,7 @@
         if j > 0:
             final_copies[j - 1].wait_recv()
         pass_copies.append(
-            send(
+            remote(
                 final.at[core, source],
                 final.at[core, source],
                 pass_sems,
@@ -1329,15 +1391,12 @@
 
     loop(slabs - 1, add_small)
 
-    for copy in pass_copies:
+    for copy in pass_copies + shares:
         copy.wait_recv()
-    half = final.shape[3]
-    for which in range(experts):
-        for side in range(2):
-            out_ref[which, :, side * half : (side + 1) * half] = final[side, which].astype(F32)
-
-    for j in range(experts):
-        core_copies[j].wait_send()
+    for copy in stores:
+        copy.wait()
+    for which in range(4):
+        core_copy(which).wait_send()
     for j in range(1, experts):
 
         def sent(k, j=j):
@@ -1345,37 +1404,50 @@
 
         loop(slabs, sent)
     loop(slabs - 1, lambda k: slab_copy(k).wait_send())
-    for copy in final_copies + pass_copies:
+    for copy in theirs + shares + final_copies + pass_copies:
         copy.wait_send()
 
 
-def reduce_shared(mesh_sizes, grads, small, gain_row, gain_at):
-    experts, slabs = mesh_sizes
-    _, _, _, rows, half = grads.shape
-    small_shape = small.shape
+def tail(experts, slabs, gain_at, sent, aone, w_shared, extra, x, dh, gwo, small, wide, down):
+    tokens, width = x.shape
+    half = width // 2
+    rows = width // slabs
     vmem = pl.BlockSpec(memory_space=pltpu.VMEM)
+    anywhere = pl.BlockSpec(memory_space=pl.ANY)
     dma = pltpu.SemaphoreType.DMA
     return pl.pallas_call(
-        functools.partial(reduce_kernel, gain_at),
-        in_specs=[vmem] * 3,
-        out_specs=[vmem] * 2,
+        functools.partial(tail_kernel, gain_at),
+        in_specs=[anywhere, vmem, anywhere, vmem, anywhere, anywhere] + [vmem] * 4,
+        out_specs=[anywhere] + [vmem] * 4,
         out_shape=(
-            jax.ShapeDtypeStruct((experts, rows, 2 * half), F32),
-            jax.ShapeDtypeStruct(small_shape, F32),
+            jax.ShapeDtypeStruct((tokens, width), F32),
+            jax.ShapeDtypeStruct((2, experts, rows, half), BF16),
+            jax.ShapeDtypeStruct(small.shape, F32),
+            jax.ShapeDtypeStruct((2,) + wide.shape, BF16),
+            jax.ShapeDtypeStruct((2,) + down.shape, BF16),
         ),
         scratch_shapes=[
-            pltpu.VMEM((experts, slabs, rows, half), BF16),
+            pltpu.VMEM((2, 3, tokens, half), BF16),
+            pltpu.VMEM((2, 4, slabs, rows, half), BF16),
+            pltpu.VMEM((3, 2, width, half), BF16),
+            pltpu.VMEM((tokens, width), BF16),
+            pltpu.VMEM((tokens, width), F32),
+            pltpu.VMEM((tokens, width), F32),
+            pltpu.VMEM((4, slabs, rows, half), BF16),
             pltpu.VMEM((experts - 1, slabs, rows, half), BF16),
             pltpu.VMEM((experts - 1, slabs, rows, half), BF16),
             pltpu.VMEM((slabs - 1, rows, half), BF16),
             pltpu.VMEM((slabs - 1, rows, half), BF16),
-            pltpu.VMEM((2, experts, rows, half), BF16),
             pltpu.VMEM((rows, half), F32),
-            pltpu.VMEM(small_shape, F32),
-            pltpu.VMEM(small_shape, F32),
-            pltpu.VMEM((experts,) + small_shape, F32),
-            pltpu.VMEM((slabs,) + small_shape, F32),
-            dma((2, experts)),
+            pltpu.VMEM(small.shape, F32),
+            pltpu.VMEM(small.shape, F32),
+            pltpu.VMEM((experts,) + small.shape, F32),
+            pltpu.VMEM((slabs,) + small.shape, F32),
+            dma((4,)),
+            dma((2,)),
+            dma((2, 3)),
+            dma((2, 2)),
+            dma((2, 4)),
             dma((2, experts - 1, slabs)),
             dma((2, slabs - 1)),
             dma((2, experts)),
@@ -1385,11 +1457,86 @@
             dma((2, slabs - 1)),
         ],
         compiler_params=pltpu.CompilerParams(
-            collective_id=0, has_side_effects=True, vmem_limit_bytes=56 * MIB
+            collective_id=0, has_side_effects=True, vmem_limit_bytes=60 * MIB
         ),
-        cost_estimate=cost(1e6, 2 * grads.size),
-        name="reduce_shared",
-    )(grads, small, gain_row)
+        cost_estimate=cost(12 * tokens * width * width, 40 * tokens * width),
+        name="tail",
+    )(sent, aone, w_shared, extra, x, dh, gwo, small, wide, down)
+
+
+def finish_kernel(
+    total,
+    slab_ref,
+    final_ref,
+    small_ref,
+    wide_ref,
+    down_ref,
+    q_ref,
+    k_ref,
+    v_ref,
+    o_ref,
+    norm_one_ref,
+    norm_two_ref,
+    router_ref,
+    mix_ref,
+    vec_ref,
+    res_ref,
+    gate_ref,
+    up_ref,
+    gd_ref,
+    turned_ref,
+):
+    rows, half = final_ref.shape[2:]
+    wide = wide_ref.shape[2] // 2
+    for which, ref in enumerate((q_ref, k_ref, v_ref, o_ref)):
+        for side in range(2):
+            ref[:, side * half : (side + 1) * half] = final_ref[side, which].astype(F32)
+    for side in range(2):
+        at = slice(side * wide, (side + 1) * wide)
+        gate_ref[0, :, at] = wide_ref[side, :, :wide].astype(F32)
+        up_ref[0, :, at] = wide_ref[side, :, wide:].astype(F32)
+        gd_ref[0, :, side * half : (side + 1) * half] = down_ref[side].astype(F32)
+    small = small_ref[...]
+    fill = jnp.zeros((LANES - small.shape[0], small.shape[1]), F32)
+    turned_ref[...] = jnp.concatenate([small, fill], axis=0).T
+    own = turned_ref[pl.ds(pl.multiple_of(slab_ref[0] * rows, 8), rows), :]
+    router_ref[...] = own[:, :total]
+    mix_ref[...] = own[:, total : total + 4]
+    norm_two_ref[...] = own[:, total + 4 : total + 5]
+    vec_ref[...] = own[:, total + 5 : total + 7]
+    norm_one_ref[...] = own[:, total + 7 : total + 8]
+    res_ref[...] = small[total + 8 :, :total]
+
+
+def finish(total, slab, final, small, wide, down):
+    rows, half = final.shape[2:]
+    width = 2 * half
+    vmem = pl.BlockSpec(memory_space=pltpu.VMEM)
+    shape = lambda *dims: jax.ShapeDtypeStruct(dims, F32)
+    return pl.pallas_call(
+        functools.partial(finish_kernel, total),
+        in_specs=[pl.BlockSpec(memory_space=pltpu.SMEM)] + [vmem] * 4,
+        out_specs=[vmem] * 13,
+        out_shape=(
+            shape(rows, width),
+            shape(rows, width),
+            shape(rows, width),
+            shape(rows, width),
+            shape(rows, 1),
+            shape(rows, 1),
+            shape(rows, total),
+            shape(rows, 4),
+            shape(rows, 2),
+            shape(total, total),
+            shape(1, rows, wide.shape[2]),
+            shape(1, rows, wide.shape[2]),
+            shape(1, down.shape[1], width),
+        ),
+        scratch_shapes=[pltpu.VMEM((width, LANES), F32)],
+        compiler_params=params(40),
+        cost_estimate=cost(1e6, 20 * rows * width),
+        name="finish",
+    )(slab, final, small, wide, down)
 
 
 def swap_cores(value):
@@ -1424,7 +1571,6 @@
     hidden = w_gate.shape[2]
     cap = (18 * rows + 8 * total - 1) // (8 * total)
     seq = 2 * rows
-    tiles = seq // TQ
     core = lax.axis_index("context")
     half = width // 2
 
@@ -1439,7 +1585,19 @@
     extra = jnp.concatenate(
         [router, const_mix, norm_one[:, None], norm_two[:, None], const_vec], axis=1
     )
-    w_shared, extra = spread(experts, dp, w_query, w_key, w_value, w_out, extra.astype(F32).T)
+    w_shared, extra, flat, flat_t, low, first = spread(
+        experts,
+        dp,
+        cap,
+        w_query,
+        w_key,
+        w_value,
+        w_out,
+        extra.astype(F32).T,
+        routes[0],
+        ranks[0],
+        segments,
+    )
     w_shared = w_shared.reshape(4, 2, width, half)
     extra = extra.transpose(1, 0, 2).reshape(total + 8, width).astype(BF16)
     extra = jnp.concatenate(
@@ -1455,12 +1613,6 @@
     up_w = gather(mine(w_up[0], hidden // 2))
     down_w = gather(mine(w_down[0], half))
 
-    flat, flat_t = place(routes[0], ranks[0, 0], experts, cap)
-    segs = lax.all_gather(segments[0], "context", axis=0, tiled=True)
-    places = jnp.arange(seq, dtype=jnp.int32)
-    starts = jnp.sum((segs[None, :] < segs[:, None]).astype(jnp.int32), axis=1)
-    low = jnp.maximum(starts, places - (WIN - 1)).reshape(tiles, 1, TQ)
-    first = low[:, 0, 0] // TQ
     cos, sin = rope_tables(seq)
     cos, sin = jnp.asarray(cos), jnp.asarray(sin)
     res = jnp.pad(w_res.astype(F32), ((0, 0), (0, LANES - total)))
@@ -1472,24 +1624,14 @@
     o_heads, lse = attend(first, qkv, low)
     o = swap_cores(o_heads)
     hres, atwo, stat = middle(total, x, o, w_shared, extra, prev_logits[0], res, routes[0])
-    flow_back, drow_back, grad_gate, grad_up, grad_down = run_experts(
+    flow_back, drow_back, grad_wide, grad_down = run_experts(
         total, experts, cap, flat_t, atwo, dy, stat, gate_w, up_w, down_w
     )
     flow_back = flow_back.reshape(experts * cap, width)
     drow_back = drow_back.reshape(experts * cap, width)
-
-    def scatter_half(chip):
-        share = lax.psum_scatter(chip, "dp", scatter_dimension=0, tiled=True)
-        both = lax.all_gather(share, "context", axis=1, tiled=True)
-        return both.astype(F32)[None]
-
-    def columns(grad):
-        return grad.transpose(1, 0, 2).reshape(width, hidden // 2)
-
-    total_gate, total_up, total_down = (
-        scatter_half(columns(grad_gate)),
-        scatter_half(columns(grad_up)),
-        scatter_half(grad_down.reshape(hidden, half)),
+    wide = lax.psum_scatter(grad_wide, "dp", scatter_dimension=0, tiled=True)
+    down = lax.psum_scatter(
+        grad_down.reshape(hidden, half), "dp", scatter_dimension=0, tiled=True
     )
 
     output, dh, dolow, grad_out_w, small = combine(
@@ -1519,34 +1661,52 @@
         cos.reshape(2, rows, LANES),
         sin.reshape(2, rows, LANES),
     )
-    grads = swap_cores(grads_sent)
-    grad_tokens, grad_shared, gain_row = project_back(grads, w_shared, extra, x, aone, dh, grad_out_w)
-    shared, small = reduce_shared(
-        (experts, dp),
-        grad_shared.reshape(2, 4, dp, width // dp, half),
+    grad_tokens, final, small, wide, down = tail(
+        experts,
+        dp,
+        total + 7,
+        grads_sent,
+        aone,
+        w_shared,
+        extra,
+        x,
+        dh,
+        grad_out_w.reshape(2, dp, width // dp, half),
         small,
-        gain_row,
-        total + 7,
-    )
-    part = width // dp
-    owned = lax.dynamic_slice_in_dim(small, lax.axis_index("dp") * part, part, 1)
-    grad_res_total = small[total + 8 :, :total]
+        wide,
+        down,
+    )
+    (
+        grad_query,
+        grad_key,
+        grad_value,
+        grad_out,
+        grad_norm_one,
+        grad_norm_two,
+        grad_router,
+        grad_mix,
+        grad_vec,
+        grad_res,
+        grad_gate,
+        grad_up,
+        grad_down,
+    ) = finish(total, lax.axis_index("dp").reshape(1), final, small, wide, down)
     return (
         output[None],
         grad_tokens[None],
-        owned[total + 7],
-        shared[0],
-        shared[1],
-        shared[2],
-        shared[3],
-        owned[total + 4],
-        owned[:total].T,
-        grad_res_total,
-        owned[total : total + 4].T,
-        owned[total + 5 : total + 7].T,
-        total_gate,
-        total_up,
-        total_down,
+        grad_norm_one[:, 0],
+        grad_query,
+        grad_key,
+        grad_value,
+        grad_out,
+        grad_norm_two[:, 0],
+        grad_router,
+        grad_res,
+        grad_mix,
+        grad_vec,
+        grad_gate,
+        grad_up,
+        grad_down,
     )
 
 

time: 515 us -> 420 us (0.82)
  Pallas kernels: 401 us -> 307 us
  waiting for transfers between devices: 2.34 us -> 37.6 us
  blocking collectives: 24.6 us -> 7.85 us
  local copies, waits for them, and re-layouts: 49 us -> 32.9 us
  starting transfers between devices: 16.1 us -> 10.5 us
    pallas_call x4 -> x3, Pallas kernels: 151 us -> 102 us  [the longest x1 63.3 us: tail(): pl.pallas_call(functools.partial(tail_kernel, gain_at), in_specs=[anywher...]
    pallas_call x1, Pallas kernels: 63.4 us -> 40.8 us  [attend_back(): pl.pallas_call(attend_back_kernel, grid_spec=pltpu.PrefetchScalarGridSpec...]
    pallas_call x1, Pallas kernels: 50.8 us -> 29.8 us  [attend(): pl.pallas_call(attend_kernel, grid_spec=pltpu.PrefetchScalarGridSpec(num_...]
    reduce_scatter x1 -> x2, waiting for transfers between devices: 0.01 us -> 18.3 us  [the longest x1 18.3 us: on_device(): wide = lax.psum_scatter(grad_wide, 'dp', scatter_dimension=0, tiled=True)]
    all_gather x3, waiting for transfers between devices: 0.01 us -> 15.6 us  [gather(): lax.all_gather(shard, ('context', 'dp'), axis=0)]
    all_gather x4 -> x0, blocking collectives: 11.9 us -> none  [the longest x3 7.68 us: scatter_half(): both = lax.all_gather(share, 'context', axis=1, tiled=True)]
    transpose x5 -> x0, local copies, waits for them, and re-layouts: 7.54 us -> none  [the longest x2 3.43 us: columns(): return grad.transpose(1, 0, 2).reshape(width, hidden // 2)]
    all_to_all x3 -> x2, starting transfers between devices: 16 us -> 9.95 us  [swap_cores(): lax.all_to_all(value, 'context', split_axis=0, concat_axis=0, tiled=True)]
  transfers between devices with their start and end apart: 9 -> 7, of which waited for: 1 -> 4; matrix products, arithmetic and copies ran while one was open for 5% -> 1% of each run, Pallas kernels for 61% -> 37%
where the time goes in v1:
time: 420 us; the launch traced here: 412 us
  Pallas kernels  307 us (73%)
  waiting for transfers between devices  37.6 us (9%)
  local copies, waits for them, and re-layouts  32.9 us (8%)
  between operations  14.7 us (4%)
  starting transfers between devices  10.5 us (2%)
  blocking collectives  7.85 us (2%)
    pallas_call x1, Pallas kernels, run_experts(): pl.pallas_call(functools.partial(expert_kernel, total), in_specs=[vmem] *...  87 us
    pallas_call x1, Pallas kernels, tail(): pl.pallas_call(functools.partial(tail_kernel, gain_at), in_specs=[anywher...  63.3 us
    pallas_call x1, Pallas kernels, attend_back(): pl.pallas_call(attend_back_kernel, grid_spec=pltpu.PrefetchScalarGridSpec...  40.8 us
    pallas_call x1, Pallas kernels, spread(): pl.pallas_call(functools.partial(spread_kernel, cap), in_specs=[vmem] * 8...  35.5 us
    pallas_call x1, Pallas kernels, combine(): pl.pallas_call(functools.partial(combine_kernel, experts, total), grid=(r...  34.2 us
    pallas_call x1, Pallas kernels, attend(): pl.pallas_call(attend_kernel, grid_spec=pltpu.PrefetchScalarGridSpec(num_...  29.8 us
    unnamed x90, local copies, waits for them, and re-layouts  29 us
    reduce_scatter x1, waiting for transfers between devices, on_device(): wide = lax.psum_scatter(grad_wide, 'dp', scatter_dimension=0, tiled=True)  18.3 us
  transfers between devices with their start and end apart: 7, of which 4 were waited for; matrix products, arithmetic and copies ran while one was open for 1% of the time, Pallas kernels for 37%

profile of v1, /device:TPU:19, one launch (start us, length us, event | category | flops | bytes accessed | tf_op | source)
XLA Modules:
  0.0 411.8 jit_solution(1738556616625033955)
XLA Ops:
  7.3 1.1 copy-done
  9.3 1.9 constant_dynamic-slice_fusion.2
  12.7 35.5 %spread.1 = (bf16[4,2,4,192,384]{4,3,2,1,0:T(8,128)(2,1)S(1)}, f32[4,16,192]{2,1,0:T(8,128)S(1)}, s32[1024,128]{1,0:T(8,128)S(1)}, f32[8,1024]{1,0:T(8,128)S(1)}...) custom-call(bf16[192,768]{1,0:T(8,128)(2,1)S(1)} %copy-done.16, bf16[192,768]{1,0:T(8,128)(2,1)S(1)} %copy-done.17, ...), custom_call_target="tpu_custom_call" | custom-call | flops 1000000 | bytes 9437184 | tf_op jit(solution)/shard_map/spread/pallas_call | solution.py:257
  48.2 2.2 copy-done.5
  51.6 1.3 copy-done.30
  52.9 1.2 copy-done.31
  54.1 7.6 %project.1 = (bf16[2,3,1024,384]{3,2,1,0:T(8,128)(2,1)S(1)}, bf16[1024,768]{1,0:T(8,128)(2,1)S(1)}) custom-call(s32[1]{0:T(128)} %bitcast.4.ctx_ref, bf16[1024,768]{1,0:T(8,128)(2,1)S(1)} %bitcast.32, bf16[128,768]{1,0:T(8,128)(2,1)S(1)} %maximum_maximum_fusion.extra_ref, bf16[4,2,768,384]{3,2,1,0:T(8,128)(2,1)} %bitcast.25, f32[2048,128]{1,0:T(8,128)S(1)} %copy-done.31, ...), custom_call_target="tpu_custom_call" | custom-call | flops 3623878656 | bytes 12976128 | tf_op jit(solution)/shard_map/project/pallas_call | solution.py:313
  61.7 1.2 copy-done.32
  62.9 7.9 %all_to_all.15.q_ref.k_ref.v_ref = bf16[2,3,1024,384]{3,2,1,0:T(8,128)(2,1)S(1)} all-to-all(bf16[2,3,1024,384]{3,2,1,0:T(8,128)(2,1)S(1)} %get-tuple-element.59), channel_id=1, replica_groups=mesh['expert'=4,'context'=2,'dp'=4] {'context'}, dimensions={0} | all-to-all | bytes 9437184 | tf_op jit(solution)/shard_map/all_to_all | solution.py:1543
  70.7 29.8 %attend.1 = (bf16[2,1024,384]{2,1,0:T(8,128)(2,1)S(1)}, f32[3,8,8,256]{3,2,1,0:T(8,128)S(1)}) custom-call(s32[8]{0:T(128)S(1)} %get-tuple-element.56.first_ref, bf16[2,3,1024,384]{3,2,1,0:T(8,128)(2,1)S(1)} %all_to_all.15.q_ref.k_ref.v_ref, bf16[2,3,1024,384]{3,2,1,0:T(8,128)(2,1)S(1)} %all_to_all.15.q_ref.k_ref.v_ref, ...), custom_call_target="tpu_custom_call" | custom-call | flops 40000000000 | bytes 6291456 | tf_op jit(solution)/shard_map/attend/pallas_call | solution.py:419
  100.6 1.1 copy-done.8
  101.7 4.2 %all-to-all-start.1 = ((bf16[2,1024,384]{2,1,0:T(8,128)(2,1)}), bf16[2,1024,384]{2,1,0:T(8,128)(2,1)S(1)}, u32[]{:S(2)}, u32[]{:S(2)}) async-start(bf16[2,1024,384]{2,1,0:T(8,128)(2,1)} %copy-done.8), calls=%async_computation.1 | async-start | bytes 3145728 | tf_op jit(solution)/shard_map/all_to_all | solution.py:1543
  106.6 1.4 all-to-all-done.1.o_ref
  108.0 2.9 copy-done.6
  110.9 1.4 copy-done.12
  112.3 5.3 %middle.1 = (f32[1024,768]{1,0:T(8,128)S(1)}, bf16[1024,768]{1,0:T(8,128)(2,1)S(1)}, f32[1024,128]{1,0:T(8,128)S(1)}) custom-call(bf16[1024,768]{1,0:T(8,128)(2,1)S(1)} %bitcast.33, bf16[2,1024,384]{2,1,0:T(8,128)(2,1)S(1)} %all-to-all-done.1.o_ref, bf16[4,2,768,384]{3,2,1,0:T(8,128)(2,1)S(1)} %bitcast.28, ...), custom_call_target="tpu_custom_call" | custom-call | flops 1207959552 | bytes 9043968 | tf_op jit(solution)/shard_map/middle/pallas_call | solution.py:625
  117.6 1.7 copy-done.23
  119.3 1.1 copy-done.24
  121.2 15.6 %all-gather.6.cloned.1.call-done = bf16[8,192,1024]{2,1,0:T(8,128)(2,1)} async-done(((bf16[1,192,1024]{2,1,0:T(8,128)(2,1)}), bf16[8,192,1024]{2,1,0:T(8,128)(2,1)}) %all-gather.6.cloned.1.call-update) | async-done | bytes 3145744 | tf_op jit(solution)/shard_map/all_gather | solution.py:1581
  136.8 87.0 %experts.1 = (bf16[4,288,768]{2,1,0:T(8,128)(2,1)}, bf16[4,288,768]{2,1,0:T(8,128)(2,1)}, bf16[768,2048]{1,0:T(8,128)(2,1)}, bf16[8,256,384]{2,1,0:T(8,128)(2,1)}) custom-call(f32[8,1024]{1,0:T(8,128)} %copy-done.27, bf16[1024,768]{1,0:T(8,128)(2,1)} %copy-done.24, bf16[1024,768]{1,0:T(8,128)(2,1)} %bitcast.41, f32[1024,128]{1,0:T(8,128)} %copy-done.26, ...), custom_call_target="tpu_custom_call" | custom-call | flops 32614907904 | bytes 47185920 | tf_op jit(solution)/shard_map/experts/pallas_call | solution.py:921
  223.8 34.2 %combine.1 = (bf16[1024,768]{1,0:T(8,128)(2,1)}, f32[1024,768]{1,0:T(8,128)}, bf16[2,1024,384]{2,1,0:T(8,128)(2,1)}, bf16[2,768,384]{2,1,0:T(8,128)(2,1)}, f32[24,768]{1,0:T(8,128)}) custom-call(bf16[1152,768]{1,0:T(8,128)(2,1)} %bitcast.43, bf16[1152,768]{1,0:T(8,128)(2,1)} %bitcast.44, s32[1024,128]{1,0:T(8,128)} %copy-done.25, f32[1024,128]{1,0:T(8,128)} %copy-done.26, ...), custom_call_target="tpu_custom_call" | custom-call | flops 7851737088 | bytes 28311552 | tf_op jit(solution)/shard_map/combine/pallas_call | solution.py:1092
  258.0 5.8 %all-to-all-start.2 = ((bf16[2,1024,384]{2,1,0:T(8,128)(2,1)}), bf16[2,1024,384]{2,1,0:T(8,128)(2,1)}, u32[]{:S(2)}, u32[]{:S(2)}) async-start(bf16[2,1024,384]{2,1,0:T(8,128)(2,1)} %get-tuple-element.69), calls=%async_computation.2 | async-start | bytes 3145728 | tf_op jit(solution)/shard_map/all_to_all | solution.py:1543
  264.4 1.7 all-to-all-done.2.do_ref
  266.1 1.2 copy-done.29
  267.3 40.8 %attend_back.1.sent_ref = bf16[2,3,1024,384]{3,2,1,0:T(8,128)(2,1)} custom-call(s32[8]{0:T(128)S(1)} %get-tuple-element.56.first_ref, bf16[2,3,1024,384]{3,2,1,0:T(8,128)(2,1)} %copy-done.4, bf16[2,3,1024,384]{3,2,1,0:T(8,128)(2,1)} %copy-done.4, bf16[2,3,1024,384]{3,2,1,0:T(8,128)(2,1)} %copy-done.4, bf16[2,1024,384]{2,1,0:T(8,128)(2,1)} %all-to-all-done.2.do_ref, ...), custom_call_target="tpu_custom_call" | custom-call | flops 99999997952 | bytes 12582912 | tf_op jit(solution)/shard_map/attend_back/pallas_call | solution.py:551
  308.1 18.3 %reduce-scatter.3.cloned.1.call-done.wide_ref = bf16[192,2048]{1,0:T(8,128)(2,1)} async-done(((bf16[768,2048]{1,0:T(8,128)(2,1)}), bf16[192,2048]{1,0:T(8,128)(2,1)}) %reduce-scatter.3.cloned.1.call-update) | async-done | bytes 786448 | tf_op jit(solution)/shard_map/reduce_scatter | solution.py:1632
  326.4 63.3 %tail.1 = (f32[1024,768]{1,0:T(8,128)}, bf16[2,4,192,384]{3,2,1,0:T(8,128)(2,1)}, f32[24,768]{1,0:T(8,128)}, bf16[2,192,2048]{2,1,0:T(8,128)(2,1)}, bf16[2,512,384]{2,1,0:T(8,128)(2,1)}) custom-call(bf16[2,3,1024,384]{3,2,1,0:T(8,128)(2,1)} %attend_back.1.sent_ref, bf16[1024,768]{1,0:T(8,128)(2,1)} %copy-done.32, bf16[4,2,768,384]{3,2,1,0:T(8,128)(2,1)} %bitcast.27, ...), custom_call_target="tpu_custom_call" | custom-call | flops 7247757312 | bytes 31457280 | tf_op jit(solution)/shard_map/tail/pallas_call | solution.py:1418
  389.7 1.4 copy-done.10
  391.1 1.3 copy-done.13
  392.4 1.1 copy-done.14
  394.4 3.3 finish.1
  401.0 3.8 copy.58
  (108 shorter events, 9.7 us)
Async XLA Ops:
  7.2 4.0 copy-start.33
  7.2 114.0 %all-gather.8.cloned.1.call-start = ((), (), s32[]{:S(2)}) async-start(), calls=%async_computation.7 | async-start | bytes 3538944 | tf_op jit(solution)/shard_map/all_gather | solution.py:1581
  9.1 3.1 copy-start.40
  9.1 3.2 copy-start.41
  9.1 3.2 copy-start.35
  9.1 3.4 copy-start.36
  9.1 3.4 copy-start.37
  9.1 3.4 copy-start.39
  9.2 3.4 copy-start.16
  9.2 3.4 copy-start.17
  9.2 3.4 copy-start.18
  9.2 3.4 copy-start.19
  9.2 3.4 copy-start.21
  9.2 3.4 copy-start.22
  9.2 112.0 %all-gather.4.cloned.1.call-start = ((), (), s32[]{:S(2)}) async-start(), calls=%async_computation.5 | async-start | bytes 3538944 | tf_op jit(solution)/shard_map/all_gather | solution.py:1581
  11.2 125.6 %all-gather.6.cloned.1.call-start = ((), (), s32[]{:S(2)}) async-start(), calls=%async_computation.6 | async-start | bytes 3538944 | tf_op jit(solution)/shard_map/all_gather | solution.py:1581
  12.1 39.5 %copy-start.11 = (bf16[1,1024,768]{2,1,0:T(8,128)(2,1)S(1)}, bf16[1,1024,768]{2,1,0:T(8,128)(2,1)}, u32[]{:S(2)}) copy-start(bf16[1,1024,768]{2,1,0:T(8,128)(2,1)} %param.21) | copy-start | bytes 4718596
  12.5 95.4 %copy-start.3 = (s32[1,1024,2]{2,1,0:T(8,128)}, s32[1,1024,2]{2,1,0:T(8,128)S(1)}, u32[]{:S(2)}) copy-start(s32[1,1024,2]{2,1,0:T(8,128)S(1)} %copy.50) | copy-start | bytes 24580
  51.2 10.5 %copy-start.27 = (f32[8,1024]{1,0:T(8,128)}, f32[8,1024]{1,0:T(8,128)S(1)}, u32[]{:S(2)}) copy-start(f32[8,1024]{1,0:T(8,128)S(1)} %get-tuple-element.55.flat_ref) | copy-start | bytes 98308
  51.5 56.5 %copy-start.15 = (bf16[128,768]{1,0:T(8,128)(2,1)}, bf16[128,768]{1,0:T(8,128)(2,1)S(1)}, u32[]{:S(2)}) copy-start(bf16[128,768]{1,0:T(8,128)(2,1)S(1)} %maximum_maximum_fusion.extra_ref) | copy-start | bytes 589828
  70.7 29.8 %copy-start.4 = (bf16[2,3,1024,384]{3,2,1,0:T(8,128)(2,1)}, bf16[2,3,1024,384]{3,2,1,0:T(8,128)(2,1)S(1)}, u32[]{:S(2)}) copy-start(bf16[2,3,1024,384]{3,2,1,0:T(8,128)(2,1)S(1)} %all_to_all.15.q_ref.k_ref.v_ref) | copy-start | bytes 14155780
  101.7 4.6 %copy-start.34 = (f32[1,1024,8]{1,2,0:T(8,128)S(1)}, f32[1,1024,8]{1,2,0:T(8,128)}, u32[]{:S(2)}) copy-start(f32[1,1024,8]{1,2,0:T(8,128)} %param.24) | copy-start | bytes 98308
  101.7 4.8 %copy-start.38 = (bf16[8,8]{1,0:T(8,128)(2,1)S(1)}, bf16[8,8]{1,0:T(8,128)(2,1)}, u32[]{:S(2)}) copy-start(bf16[8,8]{1,0:T(8,128)(2,1)} %param.34) | copy-start | bytes 388
  101.7 6.3 %all-to-all-start.1 = ((bf16[2,1024,384]{2,1,0:T(8,128)(2,1)}), bf16[2,1024,384]{2,1,0:T(8,128)(2,1)S(1)}, u32[]{:S(2)}, u32[]{:S(2)}) async-start(bf16[2,1024,384]{2,1,0:T(8,128)(2,1)} %copy-done.8), calls=%async_computation.1 | async-start | bytes 3145728 | tf_op jit(solution)/shard_map/all_to_all | solution.py:1543
  105.9 202.2 %reduce-scatter.5.cloned.1.call-start = ((), (), s32[]{:S(2)}) async-start(), calls=%async_computation.9 | async-start | bytes 1966080 | tf_op jit(solution)/shard_map/reduce_scatter | solution.py:1633
  106.6 11.0 %copy-start.7 = (f32[1,1024,8]{2,1,0:T(8,128)}, f32[1,1024,8]{2,1,0:T(8,128)S(1)}, u32[]{:S(2)}) copy-start(f32[1,1024,8]{2,1,0:T(8,128)S(1)} %copy.53) | copy-start | bytes 98308
  108.0 9.6 %copy-start.2 = (bf16[2,1024,384]{2,1,0:T(8,128)(2,1)}, bf16[2,1024,384]{2,1,0:T(8,128)(2,1)S(1)}, u32[]{:S(2)}) copy-start(bf16[2,1024,384]{2,1,0:T(8,128)(2,1)S(1)} %all-to-all-done.1.o_ref) | copy-start | bytes 4718596
  108.0 2.9 copy-start.6
  258.0 8.0 %all-to-all-start.2 = ((bf16[2,1024,384]{2,1,0:T(8,128)(2,1)}), bf16[2,1024,384]{2,1,0:T(8,128)(2,1)}, u32[]{:S(2)}, u32[]{:S(2)}) async-start(bf16[2,1024,384]{2,1,0:T(8,128)(2,1)} %get-tuple-element.69), calls=%async_computation.2 | async-start | bytes 3145728 | tf_op jit(solution)/shard_map/all_to_all | solution.py:1543
  263.8 62.5 %reduce-scatter.3.cloned.1.call-start = ((), (), s32[]{:S(2)}) async-start(), calls=%async_computation.8 | async-start | bytes 3932160 | tf_op jit(solution)/shard_map/reduce_scatter | solution.py:1632
  263.8 2.3 copy-start.28
  401.0 3.8 copy-start.1
  (17 other events, 22.1 us)
Sparse Core Ops, SparseCore 0:
  9.6 46.6 all-gather.7
  58.5 39.4 all-gather.3
  99.6 37.1 all-gather.5
  223.9 34.6 reduce-scatter.4
  266.6 59.6 reduce-scatter.2
